TPU v7x, 256 devices: a whole 4x4x8 slice. The times are simulated.
256 devices in a mesh: ctx: 64 (over y_hi, z, x), head: 4 (over y_lo, core).
Axes of the slice: x: 4, y: 4 (y_hi: 2, y_lo: 2; y = y_hi * 2 + y_lo), z: 8, core: 2. Of those that a mesh axis runs over, the one named last changes fastest.
Arguments:
- query_rows: bfloat16 [16384, 8192], P('ctx', 'head'), may hold values from -64 to 64, as said below
- key_rows: bfloat16 [16384, 512], P('ctx', 'head'), may hold values from -5 to 5
- value_rows: bfloat16 [16384, 512], P('ctx', 'head'), may hold values from -6 to 6
- kept_rows: int32 [64, 4, 64], P('ctx', 'head'), may hold values from 0 to 255
Outputs:
- attended: bfloat16 [16384, 8192], P(('ctx', 'head'))
Inputs may be any that keep to these rules, and one draw needn't show every extreme that they name: `query_rows`: queries in the range of the table; heads of one position may be large multiples of that position's key.
All inputs are finite; a program needn't handle non-finite values.
Results may differ from a plain program's by a relative error of at most 0.012.
Values may be sent and summed in bfloat16 or wider, within the bound.
A program may use at most 128 MiB of HBM per device.

v0:
```python
import math

import jax
import jax.numpy as jnp
from jax import lax
from jax.sharding import PartitionSpec as P


def from_root(value, axis, source):
    kept = jnp.where(lax.axis_index(axis) == source, value, 0).astype(value.dtype)
    return lax.psum(kept, axis)


def fresh_status(row_count, head_dim):
    return (
        jnp.zeros((row_count, head_dim), jnp.float32),
        jnp.full((row_count,), -jnp.inf, jnp.float32),
        jnp.zeros((row_count,), jnp.float32),
    )


def absorb(status, query_mat, packed_keys, allowed, factor):
    summed, largest, totals = status
    head_dim = query_mat.shape[1]
    scores = (
        lax.dot_general(
            query_mat,
            packed_keys[:, :head_dim],
            (((1,), (1,)), ((), ())),
            preferred_element_type=jnp.float32,
        )
        * factor
    )
    scores = jnp.where(allowed, scores, -jnp.inf)
    new_peak = jnp.maximum(largest, scores.max(axis=1))
    shrink = jnp.exp(largest - new_peak)
    weights = jnp.exp(scores - new_peak[:, None])
    totals = totals * shrink + weights.sum(axis=1)
    summed = summed * shrink[:, None] + jnp.dot(
        weights.astype(jnp.bfloat16), packed_keys[:, head_dim:], preferred_element_type=jnp.float32
    )
    return (summed, new_peak, totals)


def range_mask(first_row, row_count, kept_count, low_shard, high_shard):
    shard_ids = (first_row + jnp.arange(row_count, dtype=jnp.int32)) // kept_count
    return ((shard_ids >= low_shard) & (shard_ids < high_shard))[None, :]


def fold_segment(statuses, segment, first_row, task_list, kept_count, factor):
    updated = list(statuses)
    row_count = segment.shape[0]
    for offset in range(0, row_count, 512):
        portion = segment[offset : offset + 512]
        for slot_index, task_entry in enumerate(task_list):
            allowed = range_mask(
                first_row + offset, portion.shape[0], kept_count, task_entry[1], task_entry[2]
            )
            updated[slot_index] = lax.cond(
                jnp.any(allowed),
                lambda status: absorb(status, task_entry[0], portion, allowed, factor),
                lambda status: status,
                updated[slot_index],
            )
    return tuple(updated)


def per_device(query_rows, key_rows, value_rows, kept_rows):
    position = lax.axis_index("ctx")
    rows_local = key_rows.shape[0]
    head_dim = key_rows.shape[1]
    group_size = query_rows.shape[1] // head_dim
    kept_count = kept_rows.shape[2]
    factor = 1.0 / math.sqrt(head_dim)
    packed = jnp.concatenate([key_rows, value_rows], axis=1)
    anchor = from_root(packed, "ctx", 0)
    selector = (
        kept_rows[0, 0][:, None] == jnp.arange(rows_local, dtype=jnp.int32)[None, :]
    ).astype(jnp.bfloat16)
    compact = jnp.dot(selector, packed, preferred_element_type=jnp.float32).astype(jnp.bfloat16)
    query_mat = query_rows.reshape(rows_local * group_size, head_dim)
    query_pos = jnp.arange(rows_local * group_size, dtype=jnp.int32) // group_size
    causal = jnp.arange(rows_local, dtype=jnp.int32)[None, :] <= query_pos[:, None]
    status = absorb(
        fresh_status(rows_local * group_size, head_dim), query_mat, packed, causal, factor
    )
    status = absorb(
        status, query_mat, anchor, jnp.broadcast_to(position > 0, (1, anchor.shape[0])), factor
    )
    task_list = [(query_mat, jnp.int32(0), position)]
    statuses = (status,)
    statuses = fold_segment(
        statuses,
        lax.all_gather(compact, "ctx", axis=0, tiled=True),
        jnp.int32(0),
        task_list,
        kept_count,
        factor,
    )
    status = statuses[0]
    normed = (
        (status[0] / status[2][:, None])
        .astype(jnp.bfloat16)
        .reshape(rows_local, group_size * head_dim)
    )
    return lax.all_to_all(normed, "head", split_axis=0, concat_axis=1, tiled=True)


def solution(mesh):
    return jax.shard_map(
        per_device,
        mesh=mesh,
        in_specs=(P("ctx", "head"), P("ctx", "head"), P("ctx", "head"), P("ctx", "head", None)),
        out_specs=P(("ctx", "head"), None),
        check_vma=False,
    )
```

profile of v0, /device:TPU:241, one launch (start us, length us, event | category | flops | bytes accessed | tf_op | source)
XLA Modules:
  0.0 828.0 jit_solution(5276753311416554150)
XLA Ops:
  6.5 0.0 all-reduce.2.cloned.1.call-start
  6.5 0.9 constant_dynamic-update-slice_fusion.1
  7.4 0.9 constant_dynamic-update-slice_fusion
  8.3 0.7 broadcast_select_fusion
  8.9 0.0 all-reduce.2.cloned.1.call-update
  9.0 0.0 all-gather.2.cloned.1.call-start
  9.0 1.5 convolution_convert_fusion
  10.5 0.0 all-gather.2.cloned.1.call-update
  10.5 1.6 reshape.469
  12.1 0.7 fusion.140
  14.1 0.7 and_reduce_fusion.3
  16.1 0.7 and_reduce_fusion.5
  18.1 0.7 and_reduce_fusion.7
  20.3 1.6 fusion.142
  21.9 0.0 copy-start.7
  21.9 1.9 copy-done
  23.8 0.6 fusion.99
  24.4 568.0 %all-reduce.2.cloned.1.call-done = bf16[256,256]{1,0:T(8,128)(2,1)} async-done(((bf16[256,256]{1,0:T(8,128)(2,1)}), bf16[256,256]{1,0:T(8,128)(2,1)}) %all-reduce.2.cloned.1.call-update) | async-done | bytes 131088 | tf_op jit(solution)/shard_map/psum | solution.py:11
  592.5 1.7 fusion.143
  594.2 0.6 fusion.101
  594.8 3.4 fusion.98
  598.2 0.9 convolution_add_fusion.8
  599.2 131.7 %all-gather.2.cloned.1.call-done = bf16[4096,256]{1,0:T(8,128)(2,1)} async-done(((bf16[64,256]{1,0:T(8,128)(2,1)}), bf16[4096,256]{1,0:T(8,128)(2,1)}) %all-gather.2.cloned.1.call-update) | async-done | bytes 2097168 | tf_op jit(solution)/shard_map/all_gather | solution.py:94
  730.9 2.4 fusion.141
  733.3 7.9 conditional.8
  733.3 2.2 fusion
  735.6 2.1 fusion.1
  737.7 3.4 convolution_add_fusion
  741.2 8.1 conditional.9
  741.4 0.0 copy-start.5
  741.4 2.2 fusion.12
  743.6 2.1 fusion.13
  745.8 3.5 convolution_add_fusion.1
  749.2 7.9 conditional.10
  749.3 2.2 fusion.24
  751.5 2.1 fusion.25
  753.7 0.0 copy-done.4
  753.7 3.5 convolution_add_fusion.2
  757.1 8.1 conditional.11
  757.4 2.2 fusion.36
  759.7 2.1 fusion.37
  761.8 0.0 copy-done.3
  761.8 3.4 convolution_add_fusion.3
  765.2 7.9 conditional.12
  765.3 0.0 copy-start.2
  765.3 2.2 fusion.48
  767.6 2.1 fusion.49
  769.7 3.4 convolution_add_fusion.4
  773.1 7.3 conditional.13
  773.6 1.3 fusion.60
  774.9 2.1 fusion.61
  777.0 3.5 convolution_add_fusion.5
  780.5 8.8 %conditional.14 = ((f32[4096,128]{1,0:T(8,128)S(1)}, f32[4096]{0:T(1024)S(1)}, f32[4096]{0:T(1024)S(1)})) conditional(s32[]{:T(128)} %convert_element_type.64, (f32[4096,128]{1,0:T(8,128)S(1)}, f32[4096]{0:T(1024)S(1)}, f32[4096]{0:T(1024)S(1)}) %get-tuple-element.655, (s32[1,512]{1,0:T(1,128)S(1)}, s32[1,512]{1,0:T(1,128)S(1)}, ...), branch_computations={%region_37.38_spmd, %region_38.41_spmd.clone.clone} | conditional | flops 1097878528 | bytes 30949416 | solution.py:59
  780.6 2.2 fusion.72
  782.8 2.1 fusion.73
  784.9 4.4 convolution_add_fusion.6
  789.3 8.9 %conditional.15 = ((f32[4096,128]{1,0:T(8,128)S(1)}, f32[4096]{0:T(1024)S(1)})) conditional(s32[]{:T(128)} %convert_element_type.63, (f32[4096,128]{1,0:T(8,128)S(1)}, f32[4096]{0:T(1024)S(1)}) %tuple.67, (s32[1,512]{1,0:T(1,128)S(1)}, s32[1,512]{1,0:T(1,128)S(1)}, s32[1,512]{1,0:T(1,128)S(1)}, s32[1,512]{1,0:T(1,128)S(1)}, ...), branch_computations={%region_41.42_spmd, %region_42.45_spmd.clone.clone} | conditional | flops 1097878528 | bytes 30916640 | solution.py:59
  789.5 2.2 fusion.84
  791.7 2.1 fusion.85
  793.8 4.4 convolution_add_fusion.7
  798.2 0.7 divide_convert_fusion
  798.9 0.5 all_to_all.14
  799.4 20.5 %all_to_all.19 = bf16[4,64,2048]{2,1,0:T(8,128)(2,1)S(1)} all-to-all(bf16[4,64,2048]{2,1,0:T(8,128)(2,1)S(1)} %all_to_all.14), channel_id=1, replica_groups=mesh['ctx'=64,'head'=4] {'head'}, dimensions={0} | all-to-all | bytes 2097152 | tf_op jit(solution)/shard_map/all_to_all | solution.py:106
  819.9 1.1 copy.7
  (54 shorter events, 0.5 us)
Async XLA Ops:
  6.5 585.9 %all-reduce.2.cloned.1.call-start = ((), (), s32[]{:S(2)}) async-start(), calls=%async_computation.1 | async-start | bytes 262144 | tf_op jit(solution)/shard_map/psum | solution.py:11
  9.0 721.9 %all-gather.2.cloned.1.call-start = ((), (), s32[]{:S(2)}) async-start(), calls=%async_computation.2 | async-start | bytes 2129920 | tf_op jit(solution)/shard_map/all_gather | solution.py:94
  21.9 1.9 copy-start
  21.9 572.9 %copy-start.7 = (bf16[256,128]{1,0:T(8,128)(2,1)S(1)}, bf16[256,128]{1,0:T(8,128)(2,1)}, u32[]{:S(2)}) copy-start(bf16[256,128]{1,0:T(8,128)(2,1)} %param.22) | copy-start | bytes 196612
  592.5 2.4 copy-start.1
  592.5 5.8 copy-start.8
  733.3 4.4 copy-start.6
  741.4 4.4 copy-start.5
  749.3 4.4 copy-start.4
  757.4 4.4 copy-start.3
  765.3 4.4 copy-start.2
Sparse Core Ops, SparseCore 0:
  10.0 582.4 all-reduce.1
  596.5 134.3 all-gather.1
where the time goes:
time: 837 us; the launch traced here: 828 us
  waiting for transfers between devices  700 us (84%)
  matrix products  55.4 us (7%)
  other arithmetic  22.6 us (3%)
  blocking collectives  20.5 us (2%)
  between operations  19.1 us (2%)
  local copies, waits for them, and re-layouts  9.23 us (1%)
    psum x1, waiting for transfers between devices, from_root(): return lax.psum(kept, axis)  568 us
    all_gather x1, waiting for transfers between devices, per_device(): lax.all_gather(compact, 'ctx', axis=0, tiled=True)  132 us
    dot_general x10, matrix products, absorb(): jnp.dot(weights.astype(jnp.bfloat16), packed_keys[:, head_dim:], preferre...  33.8 us
    all_to_all x1, blocking collectives, per_device(): lax.all_to_all(normed, 'head', split_axis=0, concat_axis=1, tiled=True)  20.5 us
    dot_general x10, matrix products, absorb(): lax.dot_general(query_mat, packed_keys[:, :head_dim], (((1,), (1,)), ((),...  20.1 us
    reduce_sum x10, other arithmetic, absorb(): totals = totals * shrink + weights.sum(axis=1)  17.9 us
  transfers between devices with their start and end apart: 2, of which 2 were waited for; matrix products, arithmetic and copies ran while one was open for 2% of the time, Pallas kernels for 0%

commit v1 on v0

v1 whole, which is shorter than its diff:
```python
import functools
import math

import jax
import jax.numpy as jnp
from jax import lax
from jax.experimental import pallas as pl
from jax.experimental.pallas import tpu as pltpu
from jax.sharding import PartitionSpec as P

MESH = pl.DeviceIdType.MESH
HD = 128
BLK = 256
KEEP = 64
GROUP = 16
PAIR = 2
ITEMS = GROUP // PAIR
COLS = PAIR * BLK
FULL = 16
FULL_KEYS = FULL * KEEP
LAST_KEYS = FULL_KEYS + BLK
VROWS = 144
AROWS = 136
SCALE = math.log2(math.e) / math.sqrt(HD)
LOW = -1e30


def dot_t(a, b):
    return lax.dot_general(a, b, (((1,), (1,)), ((), ())), preferred_element_type=jnp.float32)


def kernel(
    shards, heads, q_ref, k_ref, v_ref, kept_ref, out_ref,
    compact, slots, anchor, kc, vt, s0, s1, p0, p1, mx, al, m_ref, acc_ref, obuf,
    send_sem, recv_sem, anchor_send, anchor_recv, out_send, out_recv, own_sem,
):
    me = lax.axis_index("ctx")
    head = lax.axis_index("head")
    scores, probs = (s0, s1), (p0, p1)

    barrier = pltpu.get_barrier_semaphore()

    def greet(c, carry):
        pl.semaphore_signal(barrier, inc=1, device_id=(c, head), device_id_type=MESH)
        return carry

    lax.fori_loop(0, me, greet, 0)
    for step in range(1, heads):
        peer = lax.rem(head + step, heads)
        pl.semaphore_signal(barrier, inc=1, device_id=(me, peer), device_id_type=MESH)

    chosen = (
        lax.broadcasted_iota(jnp.int32, (BLK, KEEP), 0) == kept_ref[...]
    ).astype(jnp.bfloat16)
    for part, ref in ((0, k_ref), (HD, v_ref)):
        picked = lax.dot_general(
            chosen, ref[...], (((0,), (0,)), ((), ())), preferred_element_type=jnp.float32
        )
        compact[:, part : part + HD] = picked.astype(jnp.bfloat16)

    @pl.when(me == 0)
    def _():
        anchor[:, :HD] = k_ref[...]
        anchor[:, HD:] = v_ref[...]

    slots[0:FULL] = jnp.concatenate(
        [
            jnp.broadcast_to(k_ref[0:1, :], (FULL * KEEP, HD)),
            jnp.zeros((FULL * KEEP, HD), jnp.bfloat16),
        ],
        axis=1,
    ).reshape(FULL, KEEP, 2 * HD)

    pl.semaphore_wait(barrier, shards - 1 - me + heads - 1)

    def block_copy(target):
        return pltpu.make_async_remote_copy(
            src_ref=compact,
            dst_ref=slots.at[FULL + me],
            send_sem=send_sem.at[target],
            recv_sem=recv_sem.at[me],
            device_id=(target, head),
            device_id_type=MESH,
        )

    def send_block(target, carry):
        block_copy(target).start()
        return carry

    lax.fori_loop(me + 1, shards, send_block, 0)

    def anchor_copy(stage, step, stride):
        return pltpu.make_async_remote_copy(
            src_ref=anchor,
            dst_ref=anchor,
            send_sem=anchor_send.at[stage, step - 1],
            recv_sem=anchor_recv,
            device_id=(me + step * stride, head),
            device_id_type=MESH,
        )

    def relay(stage, stride):
        for step in range(1, 4):
            anchor_copy(stage, step, stride).start()

    def wait_anchor():
        pltpu.make_async_copy(anchor, anchor, anchor_recv).wait()

    @pl.when(me == 0)
    def _():
        relay(0, 16)

    def score(item, slot, keys, own):
        q = q_ref[:, pl.ds(pl.multiple_of(item * PAIR * HD, HD), PAIR * HD)]
        q = jnp.concatenate([q[:, j * HD : (j + 1) * HD] for j in range(PAIR)], axis=0)
        s = dot_t(kc[0:keys], q) * SCALE
        if own:
            row = lax.broadcasted_iota(jnp.int32, (BLK, COLS), 0)
            col = lax.broadcasted_iota(jnp.int32, (BLK, COLS), 1)
            s = jnp.where(row <= jnp.bitwise_and(col, BLK - 1), s, LOW)
        scores[slot][0:keys] = s
        mx[slot] = jnp.broadcast_to(s.max(axis=0, keepdims=True), (8, COLS))

    def weigh(item, slot, keys, own):
        peak = mx[slot]
        if not own:
            before = m_ref[item]
            peak = jnp.maximum(before, peak)
            al[slot] = jnp.exp2(before - peak)
        m_ref[item] = peak
        probs[slot][0:keys] = jnp.exp2(scores[slot][0:keys] - peak[0:1]).astype(jnp.bfloat16)

    def mix(item, slot, keys, own):
        pv = jnp.dot(vt[:, 0:keys], probs[slot][0:keys], preferred_element_type=jnp.float32)
        pv = pv[:AROWS]
        if not own:
            pv = acc_ref[item] * al[slot, 0:1] + pv
        acc_ref[item] = pv

    def out_copy(item, step):
        peer = lax.rem(head + step, heads)
        rows = BLK // heads
        columns = pl.ds(pl.multiple_of((head * GROUP + item * PAIR) * HD, HD), PAIR * HD)
        return pltpu.make_async_remote_copy(
            src_ref=obuf.at[item, pl.ds(pl.multiple_of(peer * rows, rows), rows)],
            dst_ref=out_ref.at[:, columns],
            send_sem=out_send.at[item, step - 1],
            recv_sem=out_recv.at[item, step - 1],
            device_id=(me, peer),
            device_id_type=MESH,
        )

    def own_copy(item):
        rows = BLK // heads
        columns = pl.ds(pl.multiple_of((head * GROUP + item * PAIR) * HD, HD), PAIR * HD)
        return pltpu.make_async_copy(
            obuf.at[item, pl.ds(pl.multiple_of(head * rows, rows), rows)],
            out_ref.at[:, columns],
            own_sem.at[item],
        )

    def emit(item):
        a = acc_ref[item]
        o = (a[:HD] / a[HD : HD + 1]).T.astype(jnp.bfloat16)
        for j in range(PAIR):
            obuf[item, :, j * HD : (j + 1) * HD] = o[j * BLK : (j + 1) * BLK]
        for step in range(1, heads):
            out_copy(item, step).start()
        own_copy(item).start()

    def phase(keys, own=False, last=False):
        def mixed(item, slot):
            mix(item, slot, keys, own)
            if last:
                emit(item)

        score(0, 0, keys, own)
        weigh(0, 0, keys, own)
        score(1, 1, keys, own)

        def body(g, carry):
            t = 2 * g
            for b in range(2):
                mix(t + b, b, keys, own)
                weigh(t + b + 1, 1 - b, keys, own)
                score(t + b + 2, b, keys, own)
                if last:
                    emit(t + b)
            return carry

        lax.fori_loop(0, ITEMS // 2 - 1, body, 0)
        mixed(ITEMS - 2, 0)
        weigh(ITEMS - 1, 1, keys, own)
        mixed(ITEMS - 1, 1)

    kc[0:BLK] = k_ref[...]
    vt[0:HD, 0:BLK] = v_ref[...].T
    vt[HD:VROWS, 0:BLK] = jnp.ones((VROWS - HD, BLK), jnp.bfloat16)
    phase(BLK, own=True)

    @pl.when(lax.rem(me, 16) == 0)
    def _():
        @pl.when(me > 0)
        def _():
            wait_anchor()

        relay(1, 4)

    def wait_slot(slot, carry):
        pltpu.make_async_copy(compact, slots.at[FULL + slot], recv_sem.at[slot]).wait()
        return carry

    def load_chunk(first):
        lax.fori_loop(jnp.maximum(first, 0), first + FULL, wait_slot, 0)
        part = slots[pl.ds(first + FULL, FULL)]
        part = part.reshape(FULL_KEYS, 2 * HD)
        kc[0:FULL_KEYS] = part[:, :HD]
        valid = lax.broadcasted_iota(jnp.int32, (VROWS - HD, FULL_KEYS), 1) >= -first * KEEP
        vt[0:HD, 0:FULL_KEYS] = part[:, HD:].T
        vt[HD:VROWS, 0:FULL_KEYS] = valid.astype(jnp.bfloat16)

    full_chunks = lax.div(jnp.maximum(me - 1, 0), FULL)

    def full_chunk(j, carry):
        load_chunk(me - FULL * (j + 1))
        phase(FULL_KEYS)
        return carry

    lax.fori_loop(0, jnp.minimum(full_chunks, 1), full_chunk, 0)

    @pl.when(lax.rem(me, 4) == 0)
    def _():
        @pl.when(lax.rem(me, 16) > 0)
        def _():
            wait_anchor()

        relay(2, 1)

    lax.fori_loop(1, full_chunks, full_chunk, 0)

    @pl.when(me > 0)
    def _():
        load_chunk(me - FULL * (full_chunks + 1))

        @pl.when(lax.rem(me, 4) > 0)
        def _():
            wait_anchor()

        kc[FULL_KEYS:LAST_KEYS] = anchor[:, :HD]
        vt[0:HD, FULL_KEYS:LAST_KEYS] = anchor[:, HD:].T
        vt[HD:VROWS, FULL_KEYS:LAST_KEYS] = jnp.ones((VROWS - HD, BLK), jnp.bfloat16)
        phase(LAST_KEYS, last=True)

    @pl.when(me == 0)
    def _():
        for item in range(ITEMS):
            emit(item)

    def sent_block(target, carry):
        block_copy(target).wait_send()
        return carry

    lax.fori_loop(me + 1, shards, sent_block, 0)
    for stage, stride in ((0, 16), (1, 4), (2, 1)):
        relays = me == 0 if stage == 0 else lax.rem(me, 4 * stride) == 0

        @pl.when(relays)
        def _():
            for step in range(1, 4):
                anchor_copy(stage, step, stride).wait_send()

    for item in range(ITEMS):
        own_copy(item).wait()
        for step in range(1, heads):
            out_copy(item, step).wait()


def per_device(shards, heads, query_rows, key_rows, value_rows, kept_rows):
    vmem = pl.BlockSpec(memory_space=pltpu.VMEM)
    rows = BLK // heads
    f32, bf16, dma = jnp.float32, jnp.bfloat16, pltpu.SemaphoreType.DMA
    return pl.pallas_call(
        functools.partial(kernel, shards, heads),
        out_shape=jax.ShapeDtypeStruct((rows, heads * GROUP * HD), bf16),
        in_specs=[vmem] * 4,
        out_specs=pl.BlockSpec(memory_space=pl.ANY),
        scratch_shapes=[
            pltpu.VMEM((KEEP, 2 * HD), bf16),
            pltpu.VMEM((FULL + shards, KEEP, 2 * HD), bf16),
            pltpu.VMEM((BLK, 2 * HD), bf16),
            pltpu.VMEM((LAST_KEYS, HD), bf16),
            pltpu.VMEM((VROWS, LAST_KEYS), bf16),
            pltpu.VMEM((LAST_KEYS, COLS), f32),
            pltpu.VMEM((LAST_KEYS, COLS), f32),
            pltpu.VMEM((LAST_KEYS, COLS), bf16),
            pltpu.VMEM((LAST_KEYS, COLS), bf16),
            pltpu.VMEM((2, 8, COLS), f32),
            pltpu.VMEM((2, 8, COLS), f32),
            pltpu.VMEM((ITEMS, 8, COLS), f32),
            pltpu.VMEM((ITEMS, AROWS, COLS), f32),
            pltpu.VMEM((ITEMS, BLK, PAIR * HD), bf16),
            dma((shards,)),
            dma((shards,)),
            dma((3, 3)),
            dma,
            dma((ITEMS, heads - 1)),
            dma((ITEMS, heads - 1)),
            dma((ITEMS,)),
        ],
        compiler_params=pltpu.CompilerParams(
            collective_id=0, has_side_effects=True, vmem_limit_bytes=48 * 2**20
        ),
    )(query_rows, key_rows, value_rows, kept_rows.reshape(1, KEEP))


def solution(mesh):
    shards, heads = mesh.shape["ctx"], mesh.shape["head"]
    return jax.shard_map(
        functools.partial(per_device, shards, heads),
        mesh=mesh,
        in_specs=(P("ctx", "head"), P("ctx", "head"), P("ctx", "head"), P("ctx", "head", None)),
        out_specs=P(("ctx", "head"), None),
        check_vma=False,
    )
```

time: 837 us -> 94.2 us (0.11); the launches traced: 828 us -> 94 us
  waiting for transfers between devices: 700 us -> 0 us
  Pallas kernels: 0 us -> 89.5 us
  matrix products: 55.4 us -> 0 us
  other arithmetic: 22.6 us -> 0 us
  blocking collectives: 20.5 us -> 0 us
  between operations: 19.1 us -> 0.01 us
    psum x1 -> x0, waiting for transfers between devices: 568 us -> none  [from_root(): return lax.psum(kept, axis)]
    all_gather x1 -> x0, waiting for transfers between devices: 132 us -> none  [per_device(): lax.all_gather(compact, 'ctx', axis=0, tiled=True)]
    pallas_call x0 -> x1, Pallas kernels: none -> 89.5 us  [per_device(): pl.pallas_call(functools.partial(kernel, shards, heads), out_shape=jax.Sh...]
    dot_general x21 -> x0, matrix products: 55.4 us -> none  [the longest x10 33.8 us: absorb(): jnp.dot(weights.astype(jnp.bfloat16), packed_keys[:, head_dim:], preferre...]
    all_to_all x1 -> x0, blocking collectives: 20.5 us -> none  [per_device(): lax.all_to_all(normed, 'head', split_axis=0, concat_axis=1, tiled=True)]
    reduce_sum x10 -> x0, other arithmetic: 17.9 us -> none  [absorb(): totals = totals * shrink + weights.sum(axis=1)]
  transfers between devices with their start and end apart: 2 -> 0, of which waited for: 2 -> 0; matrix products, arithmetic and copies ran while one was open for 2% -> 0% of each run, Pallas kernels for 0% -> 0%
where the time goes in v1:
time: 94.2 us; the launch traced here: 94 us
  Pallas kernels  89.5 us (95%)
  local copies, waits for them, and re-layouts  4.53 us (5%)
    pallas_call x1, Pallas kernels, per_device(): pl.pallas_call(functools.partial(kernel, shards, heads), out_shape=jax.Sh...  89.5 us
    unnamed x9, local copies, waits for them, and re-layouts  4.53 us

profile of v1, /device:TPU:241, one launch (start us, length us, event | category | flops | bytes accessed | tf_op | source)
XLA Modules:
  0.0 94.0 jit_solution(5459126634279580744)
XLA Ops:
  0.0 0.0 copy-start.3
  0.0 0.7 copy-done.3
  0.7 0.0 copy-start
  0.7 1.2 %copy-done = bf16[256,2048]{1,0:T(8,128)(2,1)S(1)} copy-done((bf16[256,2048]{1,0:T(8,128)(2,1)S(1)}, bf16[256,2048]{1,0:T(8,128)(2,1)}, u32[]{:S(2)}) %copy-start) | copy-done | bytes 1048600
  1.9 0.0 copy-start.1
  1.9 0.8 copy-done.1
  2.7 0.0 copy-start.2
  2.7 0.8 copy-done.2
  3.6 89.5 %shard_map.46 = bf16[64,8192]{1,0:T(8,128)(2,1)S(1)} custom-call(bf16[256,2048]{1,0:T(8,128)(2,1)S(1)} %copy-done, bf16[256,128]{1,0:T(8,128)(2,1)S(1)} %copy-done.1, bf16[256,128]{1,0:T(8,128)(2,1)S(1)} %copy-done.2, s32[1,64]{1,0:T(1,128)S(1)} %bitcast.1), custom_call_target="tpu_custom_call" | custom-call | tf_op jit(solution)/shard_map/pallas_call | solution.py:282
  93.0 1.0 %copy.6 = bf16[64,8192]{1,0:T(8,128)(2,1)} copy(bf16[64,8192]{1,0:T(8,128)(2,1)S(1)} %shard_map.46) | data formatting | bytes 2097152
Async XLA Ops:
  0.0 0.7 copy-start.3
  0.7 1.2 %copy-start = (bf16[256,2048]{1,0:T(8,128)(2,1)S(1)}, bf16[256,2048]{1,0:T(8,128)(2,1)}, u32[]{:S(2)}) copy-start(bf16[256,2048]{1,0:T(8,128)(2,1)} %q_ref.1) | copy-start | bytes 3145732
  1.9 0.8 copy-start.1
  2.7 0.8 copy-start.2

commit v2 on v1

--- a/solution.py
+++ b/solution.py
@@ -16,6 +16,7 @@
 PAIR = 2
 ITEMS = GROUP // PAIR
 COLS = PAIR * BLK
+WIDTH = 4
 FULL = 16
 FULL_KEYS = FULL * KEEP
 LAST_KEYS = FULL_KEYS + BLK
@@ -30,24 +31,45 @@
 
 
 def kernel(
-    shards, heads, q_ref, k_ref, v_ref, kept_ref, out_ref,
+    shards, heads, q_hbm, k_hbm, v_hbm, kept_hbm, out_ref,
+    q_ref, k_ref, v_ref, kept_ref,
     compact, slots, anchor, kc, vt, s0, s1, p0, p1, mx, al, m_ref, acc_ref, obuf,
-    send_sem, recv_sem, anchor_send, anchor_recv, out_send, out_recv, own_sem,
+    load_sem, send_sem, recv_sem, relay_send, anchor_send, anchor_recv, out_send, out_recv, own_sem,
 ):
     me = lax.axis_index("ctx")
     head = lax.axis_index("head")
+    rows = shards // WIDTH
+    row, col = lax.div(me, WIDTH), lax.rem(me, WIDTH)
     scores, probs = (s0, s1), (p0, p1)
 
     barrier = pltpu.get_barrier_semaphore()
 
-    def greet(c, carry):
-        pl.semaphore_signal(barrier, inc=1, device_id=(c, head), device_id_type=MESH)
-        return carry
-
-    lax.fori_loop(0, me, greet, 0)
+    def greet(block, to_head):
+        pl.semaphore_signal(barrier, inc=1, device_id=(block, to_head), device_id_type=MESH)
+
+    def mate(step):
+        return row * WIDTH + lax.rem(col + step, WIDTH)
+
+    def greet_row(r, carry):
+        greet(r * WIDTH + col, head)
+        return carry
+
+    lax.fori_loop(0, row, greet_row, 0)
+    for step in range(1, WIDTH):
+        greet(mate(step), head)
     for step in range(1, heads):
-        peer = lax.rem(head + step, heads)
-        pl.semaphore_signal(barrier, inc=1, device_id=(me, peer), device_id_type=MESH)
+        greet(me, lax.rem(head + step, heads))
+
+    loads = [
+        pltpu.make_async_copy(src, dst, load_sem.at[n])
+        for n, (src, dst) in enumerate(
+            ((kept_hbm, kept_ref), (k_hbm, k_ref), (v_hbm, v_ref), (q_hbm, q_ref))
+        )
+    ]
+    for load in loads:
+        load.start()
+    for load in loads[:3]:
+        load.wait()
 
     chosen = (
         lax.broadcasted_iota(jnp.int32, (BLK, KEEP), 0) == kept_ref[...]
@@ -63,31 +85,44 @@
         anchor[:, :HD] = k_ref[...]
         anchor[:, HD:] = v_ref[...]
 
-    slots[0:FULL] = jnp.concatenate(
-        [
-            jnp.broadcast_to(k_ref[0:1, :], (FULL * KEEP, HD)),
-            jnp.zeros((FULL * KEEP, HD), jnp.bfloat16),
-        ],
-        axis=1,
-    ).reshape(FULL, KEEP, 2 * HD)
-
-    pl.semaphore_wait(barrier, shards - 1 - me + heads - 1)
+    pl.semaphore_wait(barrier, rows - 1 - row + WIDTH - 1 + heads - 1)
 
     def block_copy(target):
         return pltpu.make_async_remote_copy(
             src_ref=compact,
-            dst_ref=slots.at[FULL + me],
+            dst_ref=slots.at[col, row],
             send_sem=send_sem.at[target],
-            recv_sem=recv_sem.at[me],
+            recv_sem=recv_sem.at[col, row],
             device_id=(target, head),
             device_id_type=MESH,
         )
 
-    def send_block(target, carry):
+    def send_mate(target, carry):
         block_copy(target).start()
         return carry
 
-    lax.fori_loop(me + 1, shards, send_block, 0)
+    def send_row(r, carry):
+        block_copy(r * WIDTH + col).start()
+        return carry
+
+    lax.fori_loop(me + 1, (row + 1) * WIDTH, send_mate, 0)
+    lax.fori_loop(row + 1, rows, send_row, 0)
+
+    filler = jnp.concatenate(
+        [jnp.broadcast_to(k_ref[0:1, :], (KEEP, HD)), jnp.zeros((KEEP, HD), jnp.bfloat16)], axis=1
+    )
+
+    def fill_mate(c, carry):
+        slots[c, row] = filler
+        return carry
+
+    def fill_row(r, carry):
+        for c in range(WIDTH):
+            slots[c, r] = filler
+        return carry
+
+    lax.fori_loop(col, WIDTH, fill_mate, 0)
+    lax.fori_loop(row + 1, rows, fill_row, 0)
 
     def anchor_copy(stage, step, stride):
         return pltpu.make_async_remote_copy(
@@ -99,7 +134,7 @@
             device_id_type=MESH,
         )
 
-    def relay(stage, stride):
+    def relay_anchor(stage, stride):
         for step in range(1, 4):
             anchor_copy(stage, step, stride).start()
 
@@ -108,7 +143,9 @@
 
     @pl.when(me == 0)
     def _():
-        relay(0, 16)
+        relay_anchor(0, 16)
+
+    loads[3].wait()
 
     def score(item, slot, keys, own):
         q = q_ref[:, pl.ds(pl.multiple_of(item * PAIR * HD, HD), PAIR * HD)]
@@ -139,10 +176,10 @@
 
     def out_copy(item, step):
         peer = lax.rem(head + step, heads)
-        rows = BLK // heads
+        share = BLK // heads
         columns = pl.ds(pl.multiple_of((head * GROUP + item * PAIR) * HD, HD), PAIR * HD)
         return pltpu.make_async_remote_copy(
-            src_ref=obuf.at[item, pl.ds(pl.multiple_of(peer * rows, rows), rows)],
+            src_ref=obuf.at[item, pl.ds(pl.multiple_of(peer * share, share), share)],
             dst_ref=out_ref.at[:, columns],
             send_sem=out_send.at[item, step - 1],
             recv_sem=out_recv.at[item, step - 1],
@@ -151,10 +188,10 @@
         )
 
     def own_copy(item):
-        rows = BLK // heads
+        share = BLK // heads
         columns = pl.ds(pl.multiple_of((head * GROUP + item * PAIR) * HD, HD), PAIR * HD)
         return pltpu.make_async_copy(
-            obuf.at[item, pl.ds(pl.multiple_of(head * rows, rows), rows)],
+            obuf.at[item, pl.ds(pl.multiple_of(head * share, share), share)],
             out_ref.at[:, columns],
             own_sem.at[item],
         )
@@ -204,29 +241,53 @@
         def _():
             wait_anchor()
 
-        relay(1, 4)
-
-    def wait_slot(slot, carry):
-        pltpu.make_async_copy(compact, slots.at[FULL + slot], recv_sem.at[slot]).wait()
-        return carry
-
-    def load_chunk(first):
-        lax.fori_loop(jnp.maximum(first, 0), first + FULL, wait_slot, 0)
-        part = slots[pl.ds(first + FULL, FULL)]
-        part = part.reshape(FULL_KEYS, 2 * HD)
+        relay_anchor(1, 4)
+
+    def wait_slot(c, r):
+        pltpu.make_async_copy(compact, slots.at[c, r], recv_sem.at[c, r]).wait()
+
+    def relay_copy(r, step):
+        return pltpu.make_async_remote_copy(
+            src_ref=slots.at[col, r],
+            dst_ref=slots.at[col, r],
+            send_sem=relay_send.at[r, step - 1],
+            recv_sem=recv_sem.at[col, r],
+            device_id=(mate(step), head),
+            device_id_type=MESH,
+        )
+
+    def relay(n, carry):
+        r = row - 1 - n
+        wait_slot(col, r)
+        for step in (1, 3, 2):
+            relay_copy(r, step).start()
+        return carry
+
+    lax.fori_loop(0, row, relay, 0)
+
+    def load_chunk(c):
+        part = slots[c].reshape(FULL_KEYS, 2 * HD)
         kc[0:FULL_KEYS] = part[:, :HD]
-        valid = lax.broadcasted_iota(jnp.int32, (VROWS - HD, FULL_KEYS), 1) >= -first * KEEP
+        count = row + (c < col).astype(jnp.int32)
+        valid = lax.broadcasted_iota(jnp.int32, (VROWS - HD, FULL_KEYS), 1) < count * KEEP
         vt[0:HD, 0:FULL_KEYS] = part[:, HD:].T
         vt[HD:VROWS, 0:FULL_KEYS] = valid.astype(jnp.bfloat16)
 
-    full_chunks = lax.div(jnp.maximum(me - 1, 0), FULL)
-
-    def full_chunk(j, carry):
-        load_chunk(me - FULL * (j + 1))
+    def wait_rows(c):
+        def body(r, carry):
+            wait_slot(c, r)
+            return carry
+
+        lax.fori_loop(0, row, body, 0)
+
+        @pl.when(c < col)
+        def _():
+            wait_slot(c, row)
+
+    @pl.when(me > 0)
+    def _():
+        load_chunk(col)
         phase(FULL_KEYS)
-        return carry
-
-    lax.fori_loop(0, jnp.minimum(full_chunks, 1), full_chunk, 0)
 
     @pl.when(lax.rem(me, 4) == 0)
     def _():
@@ -234,13 +295,21 @@
         def _():
             wait_anchor()
 
-        relay(2, 1)
-
-    lax.fori_loop(1, full_chunks, full_chunk, 0)
+        relay_anchor(2, 1)
 
     @pl.when(me > 0)
     def _():
-        load_chunk(me - FULL * (full_chunks + 1))
+        def chunk(step, carry):
+            c = lax.rem(col + 2 * step - 1, WIDTH)
+            wait_rows(c)
+            load_chunk(c)
+            phase(FULL_KEYS)
+            return carry
+
+        lax.fori_loop(1, 3, chunk, 0)
+        c = lax.rem(col + 2, WIDTH)
+        wait_rows(c)
+        load_chunk(c)
 
         @pl.when(lax.rem(me, 4) > 0)
         def _():
@@ -256,11 +325,22 @@
         for item in range(ITEMS):
             emit(item)
 
-    def sent_block(target, carry):
+    def sent_mate(target, carry):
         block_copy(target).wait_send()
         return carry
 
-    lax.fori_loop(me + 1, shards, sent_block, 0)
+    def sent_row(r, carry):
+        block_copy(r * WIDTH + col).wait_send()
+        return carry
+
+    def relayed(r, carry):
+        for step in range(1, WIDTH):
+            relay_copy(r, step).wait_send()
+        return carry
+
+    lax.fori_loop(me + 1, (row + 1) * WIDTH, sent_mate, 0)
+    lax.fori_loop(row + 1, rows, sent_row, 0)
+    lax.fori_loop(0, row, relayed, 0)
     for stage, stride in ((0, 16), (1, 4), (2, 1)):
         relays = me == 0 if stage == 0 else lax.rem(me, 4 * stride) == 0
 
@@ -276,17 +356,20 @@
 
 
 def per_device(shards, heads, query_rows, key_rows, value_rows, kept_rows):
-    vmem = pl.BlockSpec(memory_space=pltpu.VMEM)
-    rows = BLK // heads
+    rows, depth = BLK // heads, shards // WIDTH
     f32, bf16, dma = jnp.float32, jnp.bfloat16, pltpu.SemaphoreType.DMA
     return pl.pallas_call(
         functools.partial(kernel, shards, heads),
         out_shape=jax.ShapeDtypeStruct((rows, heads * GROUP * HD), bf16),
-        in_specs=[vmem] * 4,
+        in_specs=[pl.BlockSpec(memory_space=pl.ANY)] * 4,
         out_specs=pl.BlockSpec(memory_space=pl.ANY),
         scratch_shapes=[
+            pltpu.VMEM((BLK, GROUP * HD), bf16),
+            pltpu.VMEM((BLK, HD), bf16),
+            pltpu.VMEM((BLK, HD), bf16),
+            pltpu.VMEM((1, KEEP), jnp.int32),
             pltpu.VMEM((KEEP, 2 * HD), bf16),
-            pltpu.VMEM((FULL + shards, KEEP, 2 * HD), bf16),
+            pltpu.VMEM((WIDTH, depth, KEEP, 2 * HD), bf16),
             pltpu.VMEM((BLK, 2 * HD), bf16),
             pltpu.VMEM((LAST_KEYS, HD), bf16),
             pltpu.VMEM((VROWS, LAST_KEYS), bf16),
@@ -299,8 +382,10 @@
             pltpu.VMEM((ITEMS, 8, COLS), f32),
             pltpu.VMEM((ITEMS, AROWS, COLS), f32),
             pltpu.VMEM((ITEMS, BLK, PAIR * HD), bf16),
+            dma((4,)),
             dma((shards,)),
-            dma((shards,)),
+            dma((WIDTH, depth)),
+            dma((depth, WIDTH - 1)),
             dma((3, 3)),
             dma,
             dma((ITEMS, heads - 1)),

time: 94.2 us -> 68.8 us (0.73)
  the two profiles are of different devices: /device:TPU:241 before, /device:TPU:151 now
where the time goes in v2:
time: 68.8 us; the launch traced here: 68.5 us
  Pallas kernels  64 us (93%)
  local copies, waits for them, and re-layouts  4.53 us (7%)
    pallas_call x1, Pallas kernels, per_device(): pl.pallas_call(functools.partial(kernel, shards, heads), out_shape=jax.Sh...  64 us
    unnamed x9, local copies, waits for them, and re-layouts  4.53 us

profile of v2, /device:TPU:151, one launch (start us, length us, event | category | flops | bytes accessed | tf_op | source)
XLA Modules:
  0.0 68.5 jit_solution(13682967217767374113)
XLA Ops:
  0.0 0.0 copy-start.3
  0.0 0.7 copy-done.3
  0.7 0.0 copy-start
  0.7 1.2 %copy-done = bf16[256,2048]{1,0:T(8,128)(2,1)S(1)} copy-done((bf16[256,2048]{1,0:T(8,128)(2,1)S(1)}, bf16[256,2048]{1,0:T(8,128)(2,1)}, u32[]{:S(2)}) %copy-start) | copy-done | bytes 1048600
  1.9 0.0 copy-start.1
  1.9 0.8 %copy-done.1 = bf16[256,128]{1,0:T(8,128)(2,1)S(1)} copy-done((bf16[256,128]{1,0:T(8,128)(2,1)S(1)}, bf16[256,128]{1,0:T(8,128)(2,1)}, u32[]{:S(2)}) %copy-start.1) | copy-done | bytes 65560
  2.7 0.0 copy-start.2
  2.7 0.8 %copy-done.2 = bf16[256,128]{1,0:T(8,128)(2,1)S(1)} copy-done((bf16[256,128]{1,0:T(8,128)(2,1)S(1)}, bf16[256,128]{1,0:T(8,128)(2,1)}, u32[]{:S(2)}) %copy-start.2) | copy-done | bytes 65560
  3.6 64.0 %shard_map.46 = bf16[64,8192]{1,0:T(8,128)(2,1)S(1)} custom-call(bf16[256,2048]{1,0:T(8,128)(2,1)S(1)} %copy-done, bf16[256,128]{1,0:T(8,128)(2,1)S(1)} %copy-done.1, bf16[256,128]{1,0:T(8,128)(2,1)S(1)} %copy-done.2, s32[1,64]{1,0:T(1,128)S(1)} %bitcast.1), custom_call_target="tpu_custom_call" | custom-call | tf_op jit(solution)/shard_map/pallas_call | solution.py:361
  67.6 1.0 %copy.6 = bf16[64,8192]{1,0:T(8,128)(2,1)} copy(bf16[64,8192]{1,0:T(8,128)(2,1)S(1)} %shard_map.46) | data formatting | bytes 2097152
Async XLA Ops:
  0.0 0.7 copy-start.3
  0.7 1.2 %copy-start = (bf16[256,2048]{1,0:T(8,128)(2,1)S(1)}, bf16[256,2048]{1,0:T(8,128)(2,1)}, u32[]{:S(2)}) copy-start(bf16[256,2048]{1,0:T(8,128)(2,1)} %q_hbm.1) | copy-start | bytes 3145732
  1.9 0.8 %copy-start.1 = (bf16[256,128]{1,0:T(8,128)(2,1)S(1)}, bf16[256,128]{1,0:T(8,128)(2,1)}, u32[]{:S(2)}) copy-start(bf16[256,128]{1,0:T(8,128)(2,1)} %k_hbm.1) | copy-start | bytes 196612
  2.7 0.8 %copy-start.2 = (bf16[256,128]{1,0:T(8,128)(2,1)S(1)}, bf16[256,128]{1,0:T(8,128)(2,1)}, u32[]{:S(2)}) copy-start(bf16[256,128]{1,0:T(8,128)(2,1)} %v_hbm.1) | copy-start | bytes 196612

commit v3 on v0

v3 whole, which is shorter than its diff:
```python
import functools
import math

import jax
import jax.numpy as jnp
from jax import lax
from jax.experimental import pallas as pl
from jax.experimental.pallas import tpu as pltpu
from jax.sharding import PartitionSpec as P

MESH = pl.DeviceIdType.MESH
HD = 128
BLK = 256
KEEP = 64
GROUP = 16
PER = 4
ITEMS = GROUP // PER
COLS = PER * BLK
WIDTH = 4
SLOTS = 16
HALF = 8
KEYS = HALF * KEEP
CHUNKS = 1 + 2 * WIDTH
TAIL = 4
BUNDLE = 4
VROWS = 144
AROWS = 136
PIECE = 64
SCALE = math.log2(math.e) / math.sqrt(HD)
LOW = -1e30


def kernel(
    shards, heads, q_hbm, k_hbm, v_hbm, kept_hbm, out_ref,
    q_ref, k_ref, v_ref, kept_ref,
    compact, kv, vt, s0, s1, p0, p1, mx, al, m_ref, acc_ref, obuf,
    load_sem, send_sem, mate_send, quarter_send, column_send, single_send, bundle_send,
    mate_recv, slot_recv, bundle_recv, out_send, out_recv, own_sem,
):
    me = lax.axis_index("ctx")
    head = lax.axis_index("head")
    rows = shards // WIDTH
    row, col = lax.div(me, WIDTH), lax.rem(me, WIDTH)
    count = jnp.where(me > 0, row + 1, 0)
    bundles = lax.div(count, BUNDLE)
    scores, probs = (s0, s1), (p0, p1)

    barrier = pltpu.get_barrier_semaphore()

    def greet(block, to_head):
        pl.semaphore_signal(barrier, inc=1, device_id=(block, to_head), device_id_type=MESH)

    def mate(step):
        return row * WIDTH + lax.rem(col + step, WIDTH)

    def loop(low, high, body):
        def run(n, carry):
            body(n)
            return carry

        lax.fori_loop(low, high, run, 0)

    loop(0, row, lambda r: greet(r * WIDTH + col, head))
    for step in range(1, WIDTH):
        greet(mate(step), head)
    for step in range(1, heads):
        greet(me, lax.rem(head + step, heads))

    loads = [
        pltpu.make_async_copy(src, dst, load_sem.at[n])
        for n, (src, dst) in enumerate(
            ((kept_hbm, kept_ref), (k_hbm, k_ref), (v_hbm, v_ref), (q_hbm, q_ref))
        )
    ]
    for load in loads:
        load.start()
    for load in loads[:3]:
        load.wait()

    chosen = (
        lax.broadcasted_iota(jnp.int32, (BLK, KEEP), 0) == kept_ref[...]
    ).astype(jnp.bfloat16)
    for part, ref in ((0, k_ref), (HD, v_ref)):
        picked = lax.dot_general(
            chosen, ref[...], (((0,), (0,)), ((), ())), preferred_element_type=jnp.float32
        )
        compact[:, part : part + HD] = picked.astype(jnp.bfloat16)
    for n in range(BLK // KEEP):
        kv[0, n, :, :HD] = k_ref[n * KEEP : (n + 1) * KEEP, :]
        kv[0, n, :, HD:] = v_ref[n * KEEP : (n + 1) * KEEP, :]

    pl.semaphore_wait(barrier, rows - 1 - row + WIDTH - 1 + heads - 1)

    def remote(src, dst, send, recv, block):
        return pltpu.make_async_remote_copy(
            src_ref=src, dst_ref=dst, send_sem=send, recv_sem=recv,
            device_id=(block, head), device_id_type=MESH,
        )

    def slot_ref(c, s):
        return kv.at[1 + 2 * c + lax.div(s, HALF), lax.rem(s, HALF)]

    def bundle_ref(c, g):
        per = HALF // BUNDLE
        return kv.at[1 + 2 * c + lax.div(g, per), pl.ds(BUNDLE * lax.rem(g, per), BUNDLE)]

    def block_copy(r):
        return remote(
            compact, slot_ref(col, row + 1), send_sem.at[r], slot_recv.at[col, row + 1],
            r * WIDTH + col,
        )

    def mate_copy(c):
        return remote(
            compact, kv.at[0, 4 + col], mate_send.at[c], mate_recv.at[col], row * WIDTH + c
        )

    def quarter_copy(c):
        return remote(
            kv.at[0, c], slot_ref(c, 0), quarter_send.at[c], slot_recv.at[c, 0], c
        )

    def column_copy(source, r):
        return remote(
            source, slot_ref(col, 0), column_send.at[r], slot_recv.at[col, 0], r * WIDTH + col
        )

    loop(col + 1, WIDTH, lambda c: mate_copy(c).start())

    @pl.when(me == 0)
    def _():
        for c in range(1, WIDTH):
            quarter_copy(c).start()

    loop(0, rows - 1 - row, lambda n: block_copy(rows - 1 - n).start())

    filler = jnp.concatenate(
        [jnp.broadcast_to(k_ref[0:1, :], (KEEP, HD)), jnp.zeros((KEEP, HD), jnp.bfloat16)], axis=1
    )

    def fill_mate(c):
        kv[0, 4 + c] = filler

    def fill_slot(s):
        for c in range(WIDTH):
            kv[1 + 2 * c + lax.div(s, HALF), lax.rem(s, HALF)] = filler

    loop(col, WIDTH, fill_mate)
    loop(count, SLOTS, fill_slot)

    def wait_slot(c, s):
        pltpu.make_async_copy(compact, slot_ref(c, s), slot_recv.at[c, s]).wait()

    def single_copy(s, step):
        return remote(
            slot_ref(col, s), slot_ref(col, s), single_send.at[s, step - 1], slot_recv.at[col, s],
            mate(step),
        )

    def bundle_copy(g, step):
        return remote(
            bundle_ref(col, g), bundle_ref(col, g), bundle_send.at[g, step - 1],
            bundle_recv.at[col, g], mate(step),
        )

    def to_mates(copy, do):
        for step in (1, 3, 2):
            do(copy(step))

    def start(copy):
        copy.start()

    def zero_copy(step):
        return remote(
            kv.at[0, 0], slot_ref(0, 0), single_send.at[0, step - 1], slot_recv.at[0, 0], mate(step)
        )

    def first_copies(do):
        @pl.when(me == 0)
        def _():
            loop(1, rows, lambda r: do(column_copy(kv.at[0, 0], rows - r)))
            to_mates(zero_copy, do)

        @pl.when(jnp.logical_and(row == 0, me > 0))
        def _():
            loop(1, rows, lambda r: do(column_copy(slot_ref(col, 0), rows - r)))
            for step in (1, 3, 2):
                pl.when(mate(step) > 0)(lambda: do(single_copy(0, step)))

    @pl.when(jnp.logical_and(row == 0, me > 0))
    def _():
        wait_slot(col, 0)

    first_copies(start)

    def relay_singles():
        def one(n):
            slot = count - 1 - n
            wait_slot(col, slot)
            to_mates(functools.partial(single_copy, slot), start)

        pl.when(row > 0)(lambda: loop(0, count - BUNDLE * bundles, one))

    def relay_bundle(g):
        @pl.when(g < bundles)
        def _():
            for b in range(BUNDLE):
                wait_slot(col, BUNDLE * g + b)
            to_mates(functools.partial(bundle_copy, g), start)

    def wait_relayed(c, half):
        def many(g):
            pltpu.make_async_copy(bundle_ref(c, g), bundle_ref(c, g), bundle_recv.at[c, g]).wait()

        low = jnp.maximum(BUNDLE * bundles, HALF * half)
        loop(low, jnp.minimum(count, HALF * half + HALF), lambda s: wait_slot(c, s))
        loop(2 * half, jnp.minimum(bundles, 2 * half + 2), many)

    deep = (count > HALF).astype(jnp.int32)

    def place(p):
        k = lax.div(p - 1, 1 + deep)
        step = k + (k == 2).astype(jnp.int32) - (k == 3).astype(jnp.int32)
        half = deep * (1 - lax.rem(p - 1, 2))
        return lax.rem(col + step, WIDTH), half

    def chunk_of(p):
        c, half = place(p)
        return jnp.where(p > 0, 1 + 2 * c + half, 0)

    def load_values(chunk, limit):
        vt[chunk, 0:HD] = kv[chunk].reshape(KEYS, 2 * HD)[:, HD:].T
        valid = lax.broadcasted_iota(jnp.int32, (VROWS - HD, KEYS), 1) < limit * KEEP
        vt[chunk, HD:VROWS] = valid.astype(jnp.bfloat16)

    def load_chunk(p):
        c, half = place(p)
        pl.when(c != col)(lambda: wait_relayed(c, half))
        load_values(1 + 2 * c + half, count - HALF * half)

    chunks = 1 + WIDTH * (1 + deep)
    major = ITEMS * (chunks - TAIL)
    total = ITEMS * chunks

    def walk(t):
        late = t - major
        p = jnp.where(late < 0, lax.div(t, ITEMS), chunks - TAIL + lax.rem(late, TAIL))
        item = jnp.where(late < 0, lax.rem(t, ITEMS), lax.div(late, TAIL))
        return p, item

    def where(t):
        p, item = walk(t)
        return chunk_of(p), item

    def score(chunk, item, slot, own=False):
        keys = kv[chunk].reshape(KEYS, 2 * HD)[:, :HD]
        peaks = {}

        def part(j):
            q = q_ref[:, pl.ds(pl.multiple_of((item * PER + j) * HD, HD), HD)]
            s = SCALE * lax.dot_general(
                keys, q, (((1,), (1,)), ((), ())), preferred_element_type=jnp.float32
            )
            if own:
                key = lax.broadcasted_iota(jnp.int32, (BLK, BLK), 0)
                pos = lax.broadcasted_iota(jnp.int32, (BLK, BLK), 1)
                s = jnp.concatenate([jnp.where(key <= pos, s[:BLK], LOW), s[BLK:]], axis=0)
            scores[slot][:, j * BLK : (j + 1) * BLK] = s
            peaks[j] = s.reshape(KEYS // 8, 8, BLK).max(axis=0)

        def finish():
            for j in range(PER):
                peak = peaks[j].max(axis=0, keepdims=True)
                mx[slot, :, j * BLK : (j + 1) * BLK] = jnp.broadcast_to(peak, (8, BLK))

        return [functools.partial(part, j) for j in range(PER)], finish

    def weigh(item, slot, own=False):
        peak = mx[slot]
        if not own:
            before = m_ref[item]
            peak = jnp.maximum(before, peak)
            al[slot] = jnp.exp2(before - peak)
        m_ref[item] = peak

        def part(o):
            d = scores[slot][o : o + PIECE] - peak[0:1]
            probs[slot][o : o + PIECE] = jnp.exp2(d).astype(jnp.bfloat16)

        return [functools.partial(part, o) for o in range(0, KEYS, PIECE)]

    def mix(chunk, item, slot, own=False):
        def part(j):
            here = slice(j * BLK, (j + 1) * BLK)
            pv = jnp.dot(vt[chunk], probs[slot][:, here], preferred_element_type=jnp.float32)
            pv = pv[:AROWS]
            if not own:
                pv = acc_ref[item, :, here] * al[slot, 0:1, here] + pv
            acc_ref[item, :, here] = pv

        return [functools.partial(part, j) for j in range(PER)]

    def together(a, b, c):
        parts = []
        for order, group in enumerate((a, b, c)):
            for n, part in enumerate(group):
                parts.append(((n + 0.5) / len(group), order, part))
        for _, _, part in sorted(parts, key=lambda x: x[:2]):
            part()

    share = BLK // heads

    def out_columns(item):
        return pl.ds(pl.multiple_of((head * GROUP + item * PER) * HD, HD), PER * HD)

    def out_copy(item, step):
        peer = lax.rem(head + step, heads)
        return pltpu.make_async_remote_copy(
            src_ref=obuf.at[item, pl.ds(pl.multiple_of(peer * share, share), share)],
            dst_ref=out_ref.at[:, out_columns(item)],
            send_sem=out_send.at[item, step - 1],
            recv_sem=out_recv.at[item, step - 1],
            device_id=(me, peer),
            device_id_type=MESH,
        )

    def own_copy(item):
        return pltpu.make_async_copy(
            obuf.at[item, pl.ds(pl.multiple_of(head * share, share), share)],
            out_ref.at[:, out_columns(item)],
            own_sem.at[item],
        )

    def emit(item):
        for j in range(PER):
            a = acc_ref[item, :, j * BLK : (j + 1) * BLK]
            o = (a[:HD] / a[HD : HD + 1]).T.astype(jnp.bfloat16)
            obuf[item, :, j * HD : (j + 1) * HD] = o
        for step in range(1, heads):
            out_copy(item, step).start()
        own_copy(item).start()

    loads[3].wait()
    loop(0, col, lambda c: pltpu.make_async_copy(compact, kv.at[0, 4 + c], mate_recv.at[c]).wait())
    load_values(0, 4 + col)
    for t in range(ITEMS):
        a, finish = score(0, t, t % 2, own=True)
        b = weigh(t - 1, (t - 1) % 2, own=True) if t > 0 else []
        c = mix(0, t - 2, t % 2, own=True) if t > 1 else []
        together(a, b, c)
        finish()

    def pair(t, first=False):
        for n in range(2):
            p, item = walk(t + n + 2)
            pl.when(item == 0)(functools.partial(load_chunk, p))

            def step(n=n):
                a, finish = score(*where(t + n + 2), n)
                b = weigh(where(t + n + 1)[1], 1 - n, own=first and n == 0)
                c = mix(*where(t + n), n, own=first)
                together(a, b, c)
                finish()

            pl.when(t < total)(step)

    relay_singles()
    relay_bundle(3)
    relay_bundle(2)

    @pl.when(deep == 0)
    def _():
        relay_bundle(1)
        relay_bundle(0)

    pair(jnp.int32(ITEMS - 2), True)

    def body(n):
        t = 2 * n
        pl.when(jnp.logical_and(deep == 1, t == 4))(lambda: relay_bundle(1))
        pl.when(jnp.logical_and(deep == 1, t == 6))(lambda: relay_bundle(0))
        pair(t)
        done = t + 2 - major

        @pl.when(jnp.logical_and(done > 0, lax.rem(done, TAIL) == 0))
        def _():
            emit(lax.div(done, TAIL) - 1)

    loop(ITEMS // 2, lax.div(total, 2) - 1, body)
    together([], weigh(ITEMS - 1, 1), mix(*where(total - 2), 0))
    together([], [], mix(*where(total - 1), 1))
    emit(ITEMS - 1)

    def sent(copy):
        copy.wait_send()

    loop(col + 1, WIDTH, lambda c: sent(mate_copy(c)))

    @pl.when(me == 0)
    def _():
        for c in range(1, WIDTH):
            sent(quarter_copy(c))

    loop(row + 1, rows, lambda r: sent(block_copy(r)))
    first_copies(sent)

    @pl.when(row > 0)
    def _():
        loop(BUNDLE * bundles, count, lambda s: to_mates(functools.partial(single_copy, s), sent))
        loop(0, bundles, lambda g: to_mates(functools.partial(bundle_copy, g), sent))

    for item in range(ITEMS):
        own_copy(item).wait()
        for step in range(1, heads):
            out_copy(item, step).wait()


def per_device(shards, heads, query_rows, key_rows, value_rows, kept_rows):
    rows, depth = BLK // heads, shards // WIDTH
    f32, bf16, dma = jnp.float32, jnp.bfloat16, pltpu.SemaphoreType.DMA
    return pl.pallas_call(
        functools.partial(kernel, shards, heads),
        out_shape=jax.ShapeDtypeStruct((rows, heads * GROUP * HD), bf16),
        in_specs=[pl.BlockSpec(memory_space=pl.ANY)] * 4,
        out_specs=pl.BlockSpec(memory_space=pl.ANY),
        scratch_shapes=[
            pltpu.VMEM((BLK, GROUP * HD), bf16),
            pltpu.VMEM((BLK, HD), bf16),
            pltpu.VMEM((BLK, HD), bf16),
            pltpu.VMEM((1, KEEP), jnp.int32),
            pltpu.VMEM((KEEP, 2 * HD), bf16),
            pltpu.VMEM((CHUNKS, HALF, KEEP, 2 * HD), bf16),
            pltpu.VMEM((CHUNKS, VROWS, KEYS), bf16),
            pltpu.VMEM((KEYS, COLS), f32),
            pltpu.VMEM((KEYS, COLS), f32),
            pltpu.VMEM((KEYS, COLS), bf16),
            pltpu.VMEM((KEYS, COLS), bf16),
            pltpu.VMEM((2, 8, COLS), f32),
            pltpu.VMEM((2, 8, COLS), f32),
            pltpu.VMEM((ITEMS, 8, COLS), f32),
            pltpu.VMEM((ITEMS, AROWS, COLS), f32),
            pltpu.VMEM((ITEMS, BLK, PER * HD), bf16),
            dma((4,)),
            dma((depth,)),
            dma((WIDTH,)),
            dma((WIDTH,)),
            dma((depth,)),
            dma((SLOTS, WIDTH - 1)),
            dma((SLOTS // BUNDLE, WIDTH - 1)),
            dma((WIDTH,)),
            dma((WIDTH, SLOTS)),
            dma((WIDTH, SLOTS // BUNDLE)),
            dma((ITEMS, heads - 1)),
            dma((ITEMS, heads - 1)),
            dma((ITEMS,)),
        ],
        compiler_params=pltpu.CompilerParams(
            collective_id=0, has_side_effects=True, vmem_limit_bytes=48 * 2**20
        ),
    )(query_rows, key_rows, value_rows, kept_rows.reshape(1, KEEP))


def solution(mesh):
    shards, heads = mesh.shape["ctx"], mesh.shape["head"]
    return jax.shard_map(
        functools.partial(per_device, shards, heads),
        mesh=mesh,
        in_specs=(P("ctx", "head"), P("ctx", "head"), P("ctx", "head"), P("ctx", "head", None)),
        out_specs=P(("ctx", "head"), None),
        check_vma=False,
    )
```

time: 837 us -> 57.6 us (0.07)
  waiting for transfers between devices: 700 us -> 0 us
  matrix products: 55.4 us -> 0 us
  Pallas kernels: 0 us -> 52.4 us
  other arithmetic: 22.6 us -> 0 us
  blocking collectives: 20.5 us -> 0 us
  between operations: 19.1 us -> 0.01 us
    psum x1 -> x0, waiting for transfers between devices: 568 us -> none  [from_root(): return lax.psum(kept, axis)]
    all_gather x1 -> x0, waiting for transfers between devices: 132 us -> none  [per_device(): lax.all_gather(compact, 'ctx', axis=0, tiled=True)]
    dot_general x21 -> x0, matrix products: 55.4 us -> none  [the longest x10 33.8 us: absorb(): jnp.dot(weights.astype(jnp.bfloat16), packed_keys[:, head_dim:], preferre...]
    pallas_call x0 -> x1, Pallas kernels: none -> 52.4 us  [per_device(): pl.pallas_call(functools.partial(kernel, shards, heads), out_shape=jax.Sh...]
    all_to_all x1 -> x0, blocking collectives: 20.5 us -> none  [per_device(): lax.all_to_all(normed, 'head', split_axis=0, concat_axis=1, tiled=True)]
    reduce_sum x10 -> x0, other arithmetic: 17.9 us -> none  [absorb(): totals = totals * shrink + weights.sum(axis=1)]
  transfers between devices with their start and end apart: 2 -> 0, of which waited for: 2 -> 0; matrix products, arithmetic and copies ran while one was open for 2% -> 0% of each run, Pallas kernels for 0% -> 0%
where the time goes in v3:
time: 57.6 us; the launch traced here: 56.9 us
  Pallas kernels  52.4 us (91%)
  local copies, waits for them, and re-layouts  4.53 us (8%)
    pallas_call x1, Pallas kernels, per_device(): pl.pallas_call(functools.partial(kernel, shards, heads), out_shape=jax.Sh...  52.4 us
    unnamed x9, local copies, waits for them, and re-layouts  4.53 us

profile of v3, /device:TPU:241, one launch (start us, length us, event | category | flops | bytes accessed | tf_op | source)
XLA Modules:
  0.0 56.9 jit_solution(11502786615552411653)
XLA Ops:
  0.0 0.0 copy-start.3
  0.0 0.7 %copy-done.3 = s32[1,1,64]{2,1,0:T(1,128)S(1)} copy-done((s32[1,1,64]{2,1,0:T(1,128)S(1)}, s32[1,1,64]{2,1,0:T(1,128)}, u32[]{:S(2)}) %copy-start.3) | copy-done | bytes 280
  0.7 0.0 copy-start
  0.7 1.2 %copy-done = bf16[256,2048]{1,0:T(8,128)(2,1)S(1)} copy-done((bf16[256,2048]{1,0:T(8,128)(2,1)S(1)}, bf16[256,2048]{1,0:T(8,128)(2,1)}, u32[]{:S(2)}) %copy-start) | copy-done | bytes 1048600
  1.9 0.0 copy-start.1
  1.9 0.8 %copy-done.1 = bf16[256,128]{1,0:T(8,128)(2,1)S(1)} copy-done((bf16[256,128]{1,0:T(8,128)(2,1)S(1)}, bf16[256,128]{1,0:T(8,128)(2,1)}, u32[]{:S(2)}) %copy-start.1) | copy-done | bytes 65560
  2.7 0.0 copy-start.2
  2.7 0.8 %copy-done.2 = bf16[256,128]{1,0:T(8,128)(2,1)S(1)} copy-done((bf16[256,128]{1,0:T(8,128)(2,1)S(1)}, bf16[256,128]{1,0:T(8,128)(2,1)}, u32[]{:S(2)}) %copy-start.2) | copy-done | bytes 65560
  3.6 52.4 %shard_map.46 = bf16[64,8192]{1,0:T(8,128)(2,1)S(1)} custom-call(bf16[256,2048]{1,0:T(8,128)(2,1)S(1)} %copy-done, bf16[256,128]{1,0:T(8,128)(2,1)S(1)} %copy-done.1, bf16[256,128]{1,0:T(8,128)(2,1)S(1)} %copy-done.2, s32[1,64]{1,0:T(1,128)S(1)} %bitcast.1), custom_call_target="tpu_custom_call" | custom-call | tf_op jit(solution)/shard_map/pallas_call | solution.py:421
  55.9 1.0 %copy.6 = bf16[64,8192]{1,0:T(8,128)(2,1)} copy(bf16[64,8192]{1,0:T(8,128)(2,1)S(1)} %shard_map.46) | data formatting | bytes 2097152
Async XLA Ops:
  0.0 0.7 %copy-start.3 = (s32[1,1,64]{2,1,0:T(1,128)S(1)}, s32[1,1,64]{2,1,0:T(1,128)}, u32[]{:S(2)}) copy-start(s32[1,1,64]{2,1,0:T(1,128)} %param.7) | copy-start | bytes 772
  0.7 1.2 %copy-start = (bf16[256,2048]{1,0:T(8,128)(2,1)S(1)}, bf16[256,2048]{1,0:T(8,128)(2,1)}, u32[]{:S(2)}) copy-start(bf16[256,2048]{1,0:T(8,128)(2,1)} %q_hbm.1) | copy-start | bytes 3145732
  1.9 0.8 %copy-start.1 = (bf16[256,128]{1,0:T(8,128)(2,1)S(1)}, bf16[256,128]{1,0:T(8,128)(2,1)}, u32[]{:S(2)}) copy-start(bf16[256,128]{1,0:T(8,128)(2,1)} %k_hbm.1) | copy-start | bytes 196612
  2.7 0.8 %copy-start.2 = (bf16[256,128]{1,0:T(8,128)(2,1)S(1)}, bf16[256,128]{1,0:T(8,128)(2,1)}, u32[]{:S(2)}) copy-start(bf16[256,128]{1,0:T(8,128)(2,1)} %v_hbm.1) | copy-start | bytes 196612

commit v4 on v3

--- a/solution.py
+++ b/solution.py
@@ -33,9 +33,9 @@
 def kernel(
     shards, heads, q_hbm, k_hbm, v_hbm, kept_hbm, out_ref,
     q_ref, k_ref, v_ref, kept_ref,
-    compact, kv, vt, s0, s1, p0, p1, mx, al, m_ref, acc_ref, obuf,
-    load_sem, send_sem, mate_send, quarter_send, column_send, single_send, bundle_send,
-    mate_recv, slot_recv, bundle_recv, out_send, out_recv, own_sem,
+    compact, twin, kv, vt, s0, s1, p0, p1, mx, al, m_ref, acc_ref, obuf,
+    load_sem, send_sem, mate_send, quarter_send, column_send, single_send, bundle_send, twin_send, along_send,
+    twin_recv, mate_recv, slot_recv, bundle_recv, out_send, out_recv, own_sem,
 ):
     me = lax.axis_index("ctx")
     head = lax.axis_index("head")
@@ -43,6 +43,7 @@
     row, col = lax.div(me, WIDTH), lax.rem(me, WIDTH)
     count = jnp.where(me > 0, row + 1, 0)
     bundles = lax.div(count, BUNDLE)
+    deep = (count > HALF).astype(jnp.int32)
     scores, probs = (s0, s1), (p0, p1)
 
     barrier = pltpu.get_barrier_semaphore()
@@ -65,6 +66,8 @@
         greet(mate(step), head)
     for step in range(1, heads):
         greet(me, lax.rem(head + step, heads))
+    middle = rows // 2
+    pl.when(jnp.logical_and(row == middle, col > 0))(lambda: greet(0, head))
 
     loads = [
         pltpu.make_async_copy(src, dst, load_sem.at[n])
@@ -89,7 +92,8 @@
         kv[0, n, :, :HD] = k_ref[n * KEEP : (n + 1) * KEEP, :]
         kv[0, n, :, HD:] = v_ref[n * KEEP : (n + 1) * KEEP, :]
 
-    pl.semaphore_wait(barrier, rows - 1 - row + WIDTH - 1 + heads - 1)
+    extra = jnp.where(me == 0, WIDTH - 1, 0)
+    pl.semaphore_wait(barrier, rows - 1 - row + WIDTH - 1 + heads - 1 + extra)
 
     def remote(src, dst, send, recv, block):
         return pltpu.make_async_remote_copy(
@@ -115,10 +119,17 @@
             compact, kv.at[0, 4 + col], mate_send.at[c], mate_recv.at[col], row * WIDTH + c
         )
 
-    def quarter_copy(c):
-        return remote(
-            kv.at[0, c], slot_ref(c, 0), quarter_send.at[c], slot_recv.at[c, 0], c
-        )
+    def quarter_copy(c, r):
+        return remote(
+            kv.at[0, c], slot_ref(c, 0), quarter_send.at[lax.div(r, middle), c],
+            slot_recv.at[c, 0], r * WIDTH + c,
+        )
+
+    def quarters(do):
+        for c in range(WIDTH):
+            do(quarter_copy(c, middle))
+        for c in range(1, WIDTH):
+            do(quarter_copy(c, 0))
 
     def column_copy(source, r):
         return remote(
@@ -127,12 +138,22 @@
 
     loop(col + 1, WIDTH, lambda c: mate_copy(c).start())
 
-    @pl.when(me == 0)
-    def _():
-        for c in range(1, WIDTH):
-            quarter_copy(c).start()
-
-    loop(0, rows - 1 - row, lambda n: block_copy(rows - 1 - n).start())
+    pl.when(me == 0)(lambda: quarters(lambda copy: copy.start()))
+
+    opposite = lax.rem(col + 2, WIDTH)
+    twins = jnp.logical_and(row >= HALF - 1, row < rows - 1)
+
+    def twin_copy():
+        return remote(compact, twin, twin_send, twin_recv, mate(2))
+
+    def twin_along(r):
+        return remote(
+            twin, slot_ref(opposite, row + 1), along_send.at[r], slot_recv.at[opposite, row + 1],
+            r * WIDTH + col,
+        )
+
+    pl.when(twins)(lambda: twin_copy().start())
+    loop(row + 1, rows, lambda r: block_copy(r).start())
 
     filler = jnp.concatenate(
         [jnp.broadcast_to(k_ref[0:1, :], (KEEP, HD)), jnp.zeros((KEEP, HD), jnp.bfloat16)], axis=1
@@ -167,6 +188,11 @@
         for step in (1, 3, 2):
             do(copy(step))
 
+    def to_near(copy, do):
+        for step in (1, 3):
+            do(copy(step))
+        pl.when(deep == 0)(lambda: do(copy(2)))
+
     def start(copy):
         copy.start()
 
@@ -175,54 +201,61 @@
             kv.at[0, 0], slot_ref(0, 0), single_send.at[0, step - 1], slot_recv.at[0, 0], mate(step)
         )
 
+    gives = jnp.logical_or(row == 0, row == middle)
+
     def first_copies(do):
-        @pl.when(me == 0)
-        def _():
-            loop(1, rows, lambda r: do(column_copy(kv.at[0, 0], rows - r)))
-            to_mates(zero_copy, do)
+        def along(source):
+            loop(1, middle, lambda n: do(column_copy(source, row + middle - n)))
+
+        pl.when(me == 0)(lambda: along(kv.at[0, 0]))
+        pl.when(jnp.logical_and(gives, me > 0))(lambda: along(slot_ref(col, 0)))
+
+        pl.when(me == 0)(lambda: to_mates(zero_copy, do))
 
         @pl.when(jnp.logical_and(row == 0, me > 0))
         def _():
-            loop(1, rows, lambda r: do(column_copy(slot_ref(col, 0), rows - r)))
             for step in (1, 3, 2):
                 pl.when(mate(step) > 0)(lambda: do(single_copy(0, step)))
 
-    @pl.when(jnp.logical_and(row == 0, me > 0))
+    pl.when(jnp.logical_and(gives, me > 0))(lambda: wait_slot(col, 0))
+    first_copies(start)
+
+    @pl.when(twins)
     def _():
-        wait_slot(col, 0)
-
-    first_copies(start)
+        twin_copy().wait_recv()
+        loop(row + 1, rows, lambda r: twin_along(r).start())
 
     def relay_singles():
         def one(n):
             slot = count - 1 - n
             wait_slot(col, slot)
-            to_mates(functools.partial(single_copy, slot), start)
+            to_near(functools.partial(single_copy, slot), start)
 
         pl.when(row > 0)(lambda: loop(0, count - BUNDLE * bundles, one))
 
     def relay_bundle(g):
         @pl.when(g < bundles)
         def _():
-            for b in range(BUNDLE):
+            pl.when(jnp.logical_or(g > 0, row != middle))(lambda: wait_slot(col, BUNDLE * g))
+            for b in range(1, BUNDLE):
                 wait_slot(col, BUNDLE * g + b)
-            to_mates(functools.partial(bundle_copy, g), start)
+            (to_mates if g < HALF // BUNDLE else to_near)(functools.partial(bundle_copy, g), start)
 
     def wait_relayed(c, half):
         def many(g):
             pltpu.make_async_copy(bundle_ref(c, g), bundle_ref(c, g), bundle_recv.at[c, g]).wait()
 
-        low = jnp.maximum(BUNDLE * bundles, HALF * half)
+        whole = jnp.where(jnp.logical_and(c == opposite, half == 1), HALF // BUNDLE, bundles)
+        low = jnp.maximum(BUNDLE * whole, HALF * half)
         loop(low, jnp.minimum(count, HALF * half + HALF), lambda s: wait_slot(c, s))
-        loop(2 * half, jnp.minimum(bundles, 2 * half + 2), many)
-
-    deep = (count > HALF).astype(jnp.int32)
+        loop(2 * half, jnp.minimum(whole, 2 * half + 2), many)
 
     def place(p):
-        k = lax.div(p - 1, 1 + deep)
-        step = k + (k == 2).astype(jnp.int32) - (k == 3).astype(jnp.int32)
-        half = deep * (1 - lax.rem(p - 1, 2))
-        return lax.rem(col + step, WIDTH), half
+        own = 1 + deep
+        k = lax.rem(jnp.maximum(p - 1 - own, 0), WIDTH - 1)
+        step = jnp.where(p > own, 1 + 2 * (k == 1).astype(jnp.int32) + (k == 2).astype(jnp.int32), 0)
+        late = jnp.logical_or(p == 1, jnp.logical_and(p > own, p < own + WIDTH))
+        return lax.rem(col + step, WIDTH), deep * late.astype(jnp.int32)
 
     def chunk_of(p):
         c, half = place(p)
@@ -396,18 +429,22 @@
 
     loop(col + 1, WIDTH, lambda c: sent(mate_copy(c)))
 
-    @pl.when(me == 0)
-    def _():
-        for c in range(1, WIDTH):
-            sent(quarter_copy(c))
+    pl.when(me == 0)(lambda: quarters(sent))
 
     loop(row + 1, rows, lambda r: sent(block_copy(r)))
     first_copies(sent)
 
     @pl.when(row > 0)
     def _():
-        loop(BUNDLE * bundles, count, lambda s: to_mates(functools.partial(single_copy, s), sent))
-        loop(0, bundles, lambda g: to_mates(functools.partial(bundle_copy, g), sent))
+        loop(BUNDLE * bundles, count, lambda s: to_near(functools.partial(single_copy, s), sent))
+        early = jnp.minimum(bundles, HALF // BUNDLE)
+        loop(0, early, lambda g: to_mates(functools.partial(bundle_copy, g), sent))
+        loop(early, bundles, lambda g: to_near(functools.partial(bundle_copy, g), sent))
+
+    @pl.when(twins)
+    def _():
+        twin_copy().wait_send()
+        loop(row + 1, rows, lambda r: twin_along(r).wait_send())
 
     for item in range(ITEMS):
         own_copy(item).wait()
@@ -428,6 +465,7 @@
             pltpu.VMEM((BLK, HD), bf16),
             pltpu.VMEM((BLK, HD), bf16),
             pltpu.VMEM((1, KEEP), jnp.int32),
+            pltpu.VMEM((KEEP, 2 * HD), bf16),
             pltpu.VMEM((KEEP, 2 * HD), bf16),
             pltpu.VMEM((CHUNKS, HALF, KEEP, 2 * HD), bf16),
             pltpu.VMEM((CHUNKS, VROWS, KEYS), bf16),
@@ -443,10 +481,13 @@
             dma((4,)),
             dma((depth,)),
             dma((WIDTH,)),
-            dma((WIDTH,)),
+            dma((2, WIDTH)),
             dma((depth,)),
             dma((SLOTS, WIDTH - 1)),
             dma((SLOTS // BUNDLE, WIDTH - 1)),
+            dma,
+            dma((depth,)),
+            dma,
             dma((WIDTH,)),
             dma((WIDTH, SLOTS)),
             dma((WIDTH, SLOTS // BUNDLE)),

time: 57.6 us -> 54.3 us (0.943)
  Pallas kernels: 52.4 us -> 48.9 us
    pallas_call x1, Pallas kernels: 52.4 us -> 48.9 us  [per_device(): pl.pallas_call(functools.partial(kernel, shards, heads), out_shape=jax.Sh...]
where the time goes in v4:
time: 54.3 us; the launch traced here: 53.5 us
  Pallas kernels  48.9 us (90%)
  local copies, waits for them, and re-layouts  4.53 us (8%)
    pallas_call x1, Pallas kernels, per_device(): pl.pallas_call(functools.partial(kernel, shards, heads), out_shape=jax.Sh...  48.9 us
    unnamed x9, local copies, waits for them, and re-layouts  4.53 us

profile of v4, /device:TPU:241, one launch (start us, length us, event | category | flops | bytes accessed | tf_op | source)
XLA Modules:
  0.0 53.5 jit_solution(1010310790185121528)
XLA Ops:
  0.0 0.0 copy-start.3
  0.0 0.7 %copy-done.3 = s32[1,1,64]{2,1,0:T(1,128)S(1)} copy-done((s32[1,1,64]{2,1,0:T(1,128)S(1)}, s32[1,1,64]{2,1,0:T(1,128)}, u32[]{:S(2)}) %copy-start.3) | copy-done | bytes 280
  0.7 0.0 copy-start
  0.7 1.2 %copy-done = bf16[256,2048]{1,0:T(8,128)(2,1)S(1)} copy-done((bf16[256,2048]{1,0:T(8,128)(2,1)S(1)}, bf16[256,2048]{1,0:T(8,128)(2,1)}, u32[]{:S(2)}) %copy-start) | copy-done | bytes 1048600
  1.9 0.0 copy-start.1
  1.9 0.8 %copy-done.1 = bf16[256,128]{1,0:T(8,128)(2,1)S(1)} copy-done((bf16[256,128]{1,0:T(8,128)(2,1)S(1)}, bf16[256,128]{1,0:T(8,128)(2,1)}, u32[]{:S(2)}) %copy-start.1) | copy-done | bytes 65560
  2.7 0.0 copy-start.2
  2.7 0.8 %copy-done.2 = bf16[256,128]{1,0:T(8,128)(2,1)S(1)} copy-done((bf16[256,128]{1,0:T(8,128)(2,1)S(1)}, bf16[256,128]{1,0:T(8,128)(2,1)}, u32[]{:S(2)}) %copy-start.2) | copy-done | bytes 65560
  3.6 48.9 %shard_map.46 = bf16[64,8192]{1,0:T(8,128)(2,1)S(1)} custom-call(bf16[256,2048]{1,0:T(8,128)(2,1)S(1)} %copy-done, bf16[256,128]{1,0:T(8,128)(2,1)S(1)} %copy-done.1, bf16[256,128]{1,0:T(8,128)(2,1)S(1)} %copy-done.2, s32[1,64]{1,0:T(1,128)S(1)} %bitcast.1), custom_call_target="tpu_custom_call" | custom-call | tf_op jit(solution)/shard_map/pallas_call | solution.py:458
  52.5 1.0 %copy.6 = bf16[64,8192]{1,0:T(8,128)(2,1)} copy(bf16[64,8192]{1,0:T(8,128)(2,1)S(1)} %shard_map.46) | data formatting | bytes 2097152
Async XLA Ops:
  0.0 0.7 %copy-start.3 = (s32[1,1,64]{2,1,0:T(1,128)S(1)}, s32[1,1,64]{2,1,0:T(1,128)}, u32[]{:S(2)}) copy-start(s32[1,1,64]{2,1,0:T(1,128)} %param.7) | copy-start | bytes 772
  0.7 1.2 %copy-start = (bf16[256,2048]{1,0:T(8,128)(2,1)S(1)}, bf16[256,2048]{1,0:T(8,128)(2,1)}, u32[]{:S(2)}) copy-start(bf16[256,2048]{1,0:T(8,128)(2,1)} %q_hbm.1) | copy-start | bytes 3145732
  1.9 0.8 %copy-start.1 = (bf16[256,128]{1,0:T(8,128)(2,1)S(1)}, bf16[256,128]{1,0:T(8,128)(2,1)}, u32[]{:S(2)}) copy-start(bf16[256,128]{1,0:T(8,128)(2,1)} %k_hbm.1) | copy-start | bytes 196612
  2.7 0.8 %copy-start.2 = (bf16[256,128]{1,0:T(8,128)(2,1)S(1)}, bf16[256,128]{1,0:T(8,128)(2,1)}, u32[]{:S(2)}) copy-start(bf16[256,128]{1,0:T(8,128)(2,1)} %v_hbm.1) | copy-start | bytes 196612

commit v5 on v4

--- a/solution.py
+++ b/solution.py
@@ -152,8 +152,13 @@
             r * WIDTH + col,
         )
 
+    def target(n):
+        plain = rows - 1 - n
+        turned = jnp.where(n == 2, rows - 1, jnp.where(n < 2, plain - 1, plain))
+        return jnp.where(row < rows - 3, turned, plain)
+
     pl.when(twins)(lambda: twin_copy().start())
-    loop(row + 1, rows, lambda r: block_copy(r).start())
+    loop(0, rows - 1 - row, lambda n: block_copy(target(n)).start())
 
     filler = jnp.concatenate(
         [jnp.broadcast_to(k_ref[0:1, :], (KEEP, HD)), jnp.zeros((KEEP, HD), jnp.bfloat16)], axis=1
@@ -369,7 +374,7 @@
             a = acc_ref[item, :, j * BLK : (j + 1) * BLK]
             o = (a[:HD] / a[HD : HD + 1]).T.astype(jnp.bfloat16)
             obuf[item, :, j * HD : (j + 1) * HD] = o
-        for step in range(1, heads):
+        for step in (2, 1, 3):
             out_copy(item, step).start()
         own_copy(item).start()
 

time: 54.3 us -> 53.9 us (level)
  no operation moved by 1% of the time
where the time goes in v5:
time: 53.9 us; the launch traced here: 53.5 us
  Pallas kernels  48.9 us (91%)
  local copies, waits for them, and re-layouts  4.53 us (8%)
    pallas_call x1, Pallas kernels, per_device(): pl.pallas_call(functools.partial(kernel, shards, heads), out_shape=jax.Sh...  48.9 us
    unnamed x9, local copies, waits for them, and re-layouts  4.53 us

profile of v5, /device:TPU:241, one launch (start us, length us, event | category | flops | bytes accessed | tf_op | source)
XLA Modules:
  0.0 53.5 jit_solution(16178333060902318948)
XLA Ops:
  0.0 0.0 copy-start.3
  0.0 0.7 %copy-done.3 = s32[1,1,64]{2,1,0:T(1,128)S(1)} copy-done((s32[1,1,64]{2,1,0:T(1,128)S(1)}, s32[1,1,64]{2,1,0:T(1,128)}, u32[]{:S(2)}) %copy-start.3) | copy-done | bytes 280
  0.7 0.0 copy-start
  0.7 1.2 %copy-done = bf16[256,2048]{1,0:T(8,128)(2,1)S(1)} copy-done((bf16[256,2048]{1,0:T(8,128)(2,1)S(1)}, bf16[256,2048]{1,0:T(8,128)(2,1)}, u32[]{:S(2)}) %copy-start) | copy-done | bytes 1048600
  1.9 0.0 copy-start.1
  1.9 0.8 %copy-done.1 = bf16[256,128]{1,0:T(8,128)(2,1)S(1)} copy-done((bf16[256,128]{1,0:T(8,128)(2,1)S(1)}, bf16[256,128]{1,0:T(8,128)(2,1)}, u32[]{:S(2)}) %copy-start.1) | copy-done | bytes 65560
  2.7 0.0 copy-start.2
  2.7 0.8 %copy-done.2 = bf16[256,128]{1,0:T(8,128)(2,1)S(1)} copy-done((bf16[256,128]{1,0:T(8,128)(2,1)S(1)}, bf16[256,128]{1,0:T(8,128)(2,1)}, u32[]{:S(2)}) %copy-start.2) | copy-done | bytes 65560
  3.6 48.9 %shard_map.46 = bf16[64,8192]{1,0:T(8,128)(2,1)S(1)} custom-call(bf16[256,2048]{1,0:T(8,128)(2,1)S(1)} %copy-done, bf16[256,128]{1,0:T(8,128)(2,1)S(1)} %copy-done.1, bf16[256,128]{1,0:T(8,128)(2,1)S(1)} %copy-done.2, s32[1,64]{1,0:T(1,128)S(1)} %bitcast.1), custom_call_target="tpu_custom_call" | custom-call | tf_op jit(solution)/shard_map/pallas_call | solution.py:463
  52.5 1.0 %copy.6 = bf16[64,8192]{1,0:T(8,128)(2,1)} copy(bf16[64,8192]{1,0:T(8,128)(2,1)S(1)} %shard_map.46) | data formatting | bytes 2097152
Async XLA Ops:
  0.0 0.7 %copy-start.3 = (s32[1,1,64]{2,1,0:T(1,128)S(1)}, s32[1,1,64]{2,1,0:T(1,128)}, u32[]{:S(2)}) copy-start(s32[1,1,64]{2,1,0:T(1,128)} %param.7) | copy-start | bytes 772
  0.7 1.2 %copy-start = (bf16[256,2048]{1,0:T(8,128)(2,1)S(1)}, bf16[256,2048]{1,0:T(8,128)(2,1)}, u32[]{:S(2)}) copy-start(bf16[256,2048]{1,0:T(8,128)(2,1)} %q_hbm.1) | copy-start | bytes 3145732
  1.9 0.8 %copy-start.1 = (bf16[256,128]{1,0:T(8,128)(2,1)S(1)}, bf16[256,128]{1,0:T(8,128)(2,1)}, u32[]{:S(2)}) copy-start(bf16[256,128]{1,0:T(8,128)(2,1)} %k_hbm.1) | copy-start | bytes 196612
  2.7 0.8 %copy-start.2 = (bf16[256,128]{1,0:T(8,128)(2,1)S(1)}, bf16[256,128]{1,0:T(8,128)(2,1)}, u32[]{:S(2)}) copy-start(bf16[256,128]{1,0:T(8,128)(2,1)} %v_hbm.1) | copy-start | bytes 196612

commit v6 on v5

--- a/solution.py
+++ b/solution.py
@@ -141,7 +141,7 @@
     pl.when(me == 0)(lambda: quarters(lambda copy: copy.start()))
 
     opposite = lax.rem(col + 2, WIDTH)
-    twins = jnp.logical_and(row >= HALF - 1, row < rows - 1)
+    twins = jnp.logical_and(row >= BUNDLE - 1, row < rows - 1)
 
     def twin_copy():
         return remote(compact, twin, twin_send, twin_recv, mate(2))
@@ -228,7 +228,7 @@
     @pl.when(twins)
     def _():
         twin_copy().wait_recv()
-        loop(row + 1, rows, lambda r: twin_along(r).start())
+        loop(jnp.maximum(row + 1, HALF), rows, lambda r: twin_along(r).start())
 
     def relay_singles():
         def one(n):
@@ -244,13 +244,13 @@
             pl.when(jnp.logical_or(g > 0, row != middle))(lambda: wait_slot(col, BUNDLE * g))
             for b in range(1, BUNDLE):
                 wait_slot(col, BUNDLE * g + b)
-            (to_mates if g < HALF // BUNDLE else to_near)(functools.partial(bundle_copy, g), start)
+            (to_near if g > 0 else to_mates)(functools.partial(bundle_copy, g), start)
 
     def wait_relayed(c, half):
         def many(g):
             pltpu.make_async_copy(bundle_ref(c, g), bundle_ref(c, g), bundle_recv.at[c, g]).wait()
 
-        whole = jnp.where(jnp.logical_and(c == opposite, half == 1), HALF // BUNDLE, bundles)
+        whole = jnp.where(jnp.logical_and(c == opposite, deep == 1), 1, bundles)
         low = jnp.maximum(BUNDLE * whole, HALF * half)
         loop(low, jnp.minimum(count, HALF * half + HALF), lambda s: wait_slot(c, s))
         loop(2 * half, jnp.minimum(whole, 2 * half + 2), many)
@@ -442,14 +442,14 @@
     @pl.when(row > 0)
     def _():
         loop(BUNDLE * bundles, count, lambda s: to_near(functools.partial(single_copy, s), sent))
-        early = jnp.minimum(bundles, HALF // BUNDLE)
+        early = jnp.minimum(bundles, 1)
         loop(0, early, lambda g: to_mates(functools.partial(bundle_copy, g), sent))
         loop(early, bundles, lambda g: to_near(functools.partial(bundle_copy, g), sent))
 
     @pl.when(twins)
     def _():
         twin_copy().wait_send()
-        loop(row + 1, rows, lambda r: twin_along(r).wait_send())
+        loop(jnp.maximum(row + 1, HALF), rows, lambda r: twin_along(r).wait_send())
 
     for item in range(ITEMS):
         own_copy(item).wait()

time: 53.9 us -> 54.3 us (level)
  the two profiles are of different devices: /device:TPU:241 before, /device:TPU:17 now
where the time goes in v6:
time: 54.3 us; the launch traced here: 54.1 us
  Pallas kernels  49.5 us (91%)
  local copies, waits for them, and re-layouts  4.53 us (8%)
    pallas_call x1, Pallas kernels, per_device(): pl.pallas_call(functools.partial(kernel, shards, heads), out_shape=jax.Sh...  49.5 us
    unnamed x9, local copies, waits for them, and re-layouts  4.53 us

profile of v6, /device:TPU:17, one launch (start us, length us, event | category | flops | bytes accessed | tf_op | source)
XLA Modules:
  0.0 54.1 jit_solution(15580175130806196925)
XLA Ops:
  0.0 0.0 copy-start.3
  0.0 0.7 %copy-done.3 = s32[1,1,64]{2,1,0:T(1,128)S(1)} copy-done((s32[1,1,64]{2,1,0:T(1,128)S(1)}, s32[1,1,64]{2,1,0:T(1,128)}, u32[]{:S(2)}) %copy-start.3) | copy-done | bytes 280
  0.7 0.0 copy-start
  0.7 1.2 %copy-done = bf16[256,2048]{1,0:T(8,128)(2,1)S(1)} copy-done((bf16[256,2048]{1,0:T(8,128)(2,1)S(1)}, bf16[256,2048]{1,0:T(8,128)(2,1)}, u32[]{:S(2)}) %copy-start) | copy-done | bytes 1048600
  1.9 0.0 copy-start.1
  1.9 0.8 %copy-done.1 = bf16[256,128]{1,0:T(8,128)(2,1)S(1)} copy-done((bf16[256,128]{1,0:T(8,128)(2,1)S(1)}, bf16[256,128]{1,0:T(8,128)(2,1)}, u32[]{:S(2)}) %copy-start.1) | copy-done | bytes 65560
  2.7 0.0 copy-start.2
  2.7 0.8 %copy-done.2 = bf16[256,128]{1,0:T(8,128)(2,1)S(1)} copy-done((bf16[256,128]{1,0:T(8,128)(2,1)S(1)}, bf16[256,128]{1,0:T(8,128)(2,1)}, u32[]{:S(2)}) %copy-start.2) | copy-done | bytes 65560
  3.6 49.5 %shard_map.46 = bf16[64,8192]{1,0:T(8,128)(2,1)S(1)} custom-call(bf16[256,2048]{1,0:T(8,128)(2,1)S(1)} %copy-done, bf16[256,128]{1,0:T(8,128)(2,1)S(1)} %copy-done.1, bf16[256,128]{1,0:T(8,128)(2,1)S(1)} %copy-done.2, s32[1,64]{1,0:T(1,128)S(1)} %bitcast.1), custom_call_target="tpu_custom_call" | custom-call | tf_op jit(solution)/shard_map/pallas_call | solution.py:463
  53.1 1.0 %copy.6 = bf16[64,8192]{1,0:T(8,128)(2,1)} copy(bf16[64,8192]{1,0:T(8,128)(2,1)S(1)} %shard_map.46) | data formatting | bytes 2097152
Async XLA Ops:
  0.0 0.7 %copy-start.3 = (s32[1,1,64]{2,1,0:T(1,128)S(1)}, s32[1,1,64]{2,1,0:T(1,128)}, u32[]{:S(2)}) copy-start(s32[1,1,64]{2,1,0:T(1,128)} %param.7) | copy-start | bytes 772
  0.7 1.2 %copy-start = (bf16[256,2048]{1,0:T(8,128)(2,1)S(1)}, bf16[256,2048]{1,0:T(8,128)(2,1)}, u32[]{:S(2)}) copy-start(bf16[256,2048]{1,0:T(8,128)(2,1)} %q_hbm.1) | copy-start | bytes 3145732
  1.9 0.8 %copy-start.1 = (bf16[256,128]{1,0:T(8,128)(2,1)S(1)}, bf16[256,128]{1,0:T(8,128)(2,1)}, u32[]{:S(2)}) copy-start(bf16[256,128]{1,0:T(8,128)(2,1)} %k_hbm.1) | copy-start | bytes 196612
  2.7 0.8 %copy-start.2 = (bf16[256,128]{1,0:T(8,128)(2,1)S(1)}, bf16[256,128]{1,0:T(8,128)(2,1)}, u32[]{:S(2)}) copy-start(bf16[256,128]{1,0:T(8,128)(2,1)} %v_hbm.1) | copy-start | bytes 196612

commit v7 on v5

--- a/solution.py
+++ b/solution.py
@@ -228,7 +228,7 @@
     @pl.when(twins)
     def _():
         twin_copy().wait_recv()
-        loop(row + 1, rows, lambda r: twin_along(r).start())
+        loop(0, rows - 1 - row, lambda n: twin_along(rows - 1 - n).start())
 
     def relay_singles():
         def one(n):

time: 53.9 us -> 53.9 us (level)
  no operation moved by 1% of the time
where the time goes in v7:
time: 53.9 us; the launch traced here: 53.5 us
  Pallas kernels  48.9 us (91%)
  local copies, waits for them, and re-layouts  4.53 us (8%)
    pallas_call x1, Pallas kernels, per_device(): pl.pallas_call(functools.partial(kernel, shards, heads), out_shape=jax.Sh...  48.9 us
    unnamed x9, local copies, waits for them, and re-layouts  4.53 us

profile of v7, /device:TPU:241, one launch (start us, length us, event | category | flops | bytes accessed | tf_op | source)
XLA Modules:
  0.0 53.5 jit_solution(11780387091525362739)
XLA Ops:
  0.0 0.0 copy-start.3
  0.0 0.7 %copy-done.3 = s32[1,1,64]{2,1,0:T(1,128)S(1)} copy-done((s32[1,1,64]{2,1,0:T(1,128)S(1)}, s32[1,1,64]{2,1,0:T(1,128)}, u32[]{:S(2)}) %copy-start.3) | copy-done | bytes 280
  0.7 0.0 copy-start
  0.7 1.2 %copy-done = bf16[256,2048]{1,0:T(8,128)(2,1)S(1)} copy-done((bf16[256,2048]{1,0:T(8,128)(2,1)S(1)}, bf16[256,2048]{1,0:T(8,128)(2,1)}, u32[]{:S(2)}) %copy-start) | copy-done | bytes 1048600
  1.9 0.0 copy-start.1
  1.9 0.8 %copy-done.1 = bf16[256,128]{1,0:T(8,128)(2,1)S(1)} copy-done((bf16[256,128]{1,0:T(8,128)(2,1)S(1)}, bf16[256,128]{1,0:T(8,128)(2,1)}, u32[]{:S(2)}) %copy-start.1) | copy-done | bytes 65560
  2.7 0.0 copy-start.2
  2.7 0.8 %copy-done.2 = bf16[256,128]{1,0:T(8,128)(2,1)S(1)} copy-done((bf16[256,128]{1,0:T(8,128)(2,1)S(1)}, bf16[256,128]{1,0:T(8,128)(2,1)}, u32[]{:S(2)}) %copy-start.2) | copy-done | bytes 65560
  3.6 48.9 %shard_map.46 = bf16[64,8192]{1,0:T(8,128)(2,1)S(1)} custom-call(bf16[256,2048]{1,0:T(8,128)(2,1)S(1)} %copy-done, bf16[256,128]{1,0:T(8,128)(2,1)S(1)} %copy-done.1, bf16[256,128]{1,0:T(8,128)(2,1)S(1)} %copy-done.2, s32[1,64]{1,0:T(1,128)S(1)} %bitcast.1), custom_call_target="tpu_custom_call" | custom-call | tf_op jit(solution)/shard_map/pallas_call | solution.py:463
  52.5 1.0 %copy.6 = bf16[64,8192]{1,0:T(8,128)(2,1)} copy(bf16[64,8192]{1,0:T(8,128)(2,1)S(1)} %shard_map.46) | data formatting | bytes 2097152
Async XLA Ops:
  0.0 0.7 %copy-start.3 = (s32[1,1,64]{2,1,0:T(1,128)S(1)}, s32[1,1,64]{2,1,0:T(1,128)}, u32[]{:S(2)}) copy-start(s32[1,1,64]{2,1,0:T(1,128)} %param.7) | copy-start | bytes 772
  0.7 1.2 %copy-start = (bf16[256,2048]{1,0:T(8,128)(2,1)S(1)}, bf16[256,2048]{1,0:T(8,128)(2,1)}, u32[]{:S(2)}) copy-start(bf16[256,2048]{1,0:T(8,128)(2,1)} %q_hbm.1) | copy-start | bytes 3145732
  1.9 0.8 %copy-start.1 = (bf16[256,128]{1,0:T(8,128)(2,1)S(1)}, bf16[256,128]{1,0:T(8,128)(2,1)}, u32[]{:S(2)}) copy-start(bf16[256,128]{1,0:T(8,128)(2,1)} %k_hbm.1) | copy-start | bytes 196612
  2.7 0.8 %copy-start.2 = (bf16[256,128]{1,0:T(8,128)(2,1)S(1)}, bf16[256,128]{1,0:T(8,128)(2,1)}, u32[]{:S(2)}) copy-start(bf16[256,128]{1,0:T(8,128)(2,1)} %v_hbm.1) | copy-start | bytes 196612
